TPU v7x, 32 devices: a whole 2x2x4 slice. The times are simulated.
32 devices in a mesh: gx: 8 (over z, y), gy: 4 (over x, core).
Axes of the slice: x: 2, y: 2, z: 4, core: 2. Of those that a mesh axis runs over, the one named last changes fastest.
Arguments:
- object_field: float32 [2, 2048, 4096], P(None, 'gy', 'gx'), may hold values from -6 to 6
- probe: float32 [2, 256, 256], replicated, may hold values from -4 to 4
- frames: float32 [4, 8, 8, 3, 256, 256], P('gy', 'gx'), may hold values from 0.2 to 5
- positions: int32 [4, 8, 24, 2], P('gy', 'gx'), may hold values from -128 to 384
- helpers: int32 [4, 8, 24, 1], P('gy', 'gx'), may hold values from 0 to 7; in each aligned block of 24 rows (0 to 23, 24 to 47, ..., all dimensions but the last counted through in order) at most 3 rows name the same one
- task_counts: int32 [4, 8], P('gy', 'gx'), may hold values from 6 to 24, as said below
Outputs:
- updated_field: float32 [2, 2048, 4096], P(None, 'gy', 'gx')
Inputs may be any that keep to these rules, and one draw needn't show every extreme that they name: `helpers`: among one tile's 24 task slots no helper column is named more than 3 times, and in some tiles one is named exactly 3 times. `task_counts`: some tile has all 24 tasks valid.
All inputs are finite; a program needn't handle non-finite values.
Results may differ from a plain program's by a relative error of at most 0.0003.
Values sent between devices are 32-bit elements; how exact they have to be, the bound alone decides.
A program may use at most 192 MiB of HBM per device.

v0:
```python
import jax
import jax.numpy as jnp
from jax import lax
from jax.sharding import PartitionSpec as P

PATCH = 256
TASKS = 24


step_size = 0.1
ridge = 0.5


def extended_2(block, sides, width):
    for axis, dim in sides:
        count = lax.axis_size(axis)
        forward = [(i, i + 1) for i in range(count - 1)]
        backward = [(target, source) for source, target in forward]
        low = lax.ppermute(
            lax.slice_in_dim(block, block.shape[dim] - width, None, axis=dim), axis, forward
        )
        high = lax.ppermute(lax.slice_in_dim(block, 0, width, axis=dim), axis, backward)
        block = jnp.concatenate([low, block, high], axis=dim)
    return block


def dft_tables(length):
    index = jnp.arange(length, dtype=jnp.int32)
    phase = index[:, None] * index[None, :] % length
    angle = 2.0 * jnp.pi / length * phase.astype(jnp.float32)
    factor = length ** (-0.5)
    return (jnp.cos(angle) * factor, -jnp.sin(angle) * factor)


def right_mul(real_in, imag_in, table_re, table_im):
    highest = lax.Precision.HIGHEST
    first = jnp.einsum("bij,jk->bik", real_in, table_re, precision=highest)
    second = jnp.einsum("bij,jk->bik", imag_in, table_im, precision=highest)
    third = jnp.einsum("bij,jk->bik", real_in + imag_in, table_re + table_im, precision=highest)
    return (first - second, third - first - second)


def left_mul(table_re, table_im, real_in, imag_in):
    highest = lax.Precision.HIGHEST
    first = jnp.einsum("ij,bjk->bik", table_re, real_in, precision=highest)
    second = jnp.einsum("ij,bjk->bik", table_im, imag_in, precision=highest)
    third = jnp.einsum("ij,bjk->bik", table_re + table_im, real_in + imag_in, precision=highest)
    return (first - second, third - first - second)


def transform(real_in, imag_in, table_re, table_im):
    mid_re, mid_im = right_mul(real_in, imag_in, table_re, table_im)
    return left_mul(table_re, table_im, mid_re, mid_im)


def task_grad(patches, measured, probe):
    length = patches.shape[-1]
    table_re, table_im = dft_tables(length)
    probe_re, probe_im = (probe[0], probe[1])
    obj_re, obj_im = (patches[:, 0], patches[:, 1])
    wave_re = probe_re * obj_re - probe_im * obj_im
    wave_im = probe_re * obj_im + probe_im * obj_re
    far_re, far_im = transform(wave_re, wave_im, table_re, table_im)
    weight = far_re * far_re + far_im * far_im - measured
    back_re, back_im = transform(weight * far_re, weight * far_im, table_re, -table_im)
    grad_re = probe_re * back_re + probe_im * back_im
    grad_im = probe_re * back_im - probe_im * back_re
    return jnp.stack([grad_re, grad_im], axis=1)


def per_device(object_field, probe, frames, positions, helpers, task_counts):
    tile = object_field.shape[1]
    half = PATCH // 2
    zero = jnp.int32(0)
    extended = extended_2(object_field, (("gx", 2), ("gy", 1)), half)
    offsets = positions[0, 0]
    task_ids = jnp.arange(TASKS, dtype=jnp.int32)
    valid = task_ids < task_counts[0, 0]
    helper_cols = helpers[0, 0, :, 0]
    same = helper_cols[:, None] == helper_cols[None, :]
    ranks = jnp.sum(jnp.logical_and(same, task_ids[None, :] < task_ids[:, None]), axis=1)
    kept = frames[0, 0]
    sources = kept.shape[0]
    slot_count = kept.shape[1]
    width_all = sources * slot_count
    slot_of = helper_cols * slot_count + ranks

    def cut_patch(offset):
        return lax.dynamic_slice(
            extended, (zero, offset[0] + half, offset[1] + half), (2, PATCH, PATCH)
        )

    live = valid.astype(jnp.float32)[:, None, None, None]
    patches = jax.vmap(cut_patch)(offsets) * live
    fetched = lax.all_to_all(kept, "gx", split_axis=0, concat_axis=0, tiled=True)
    measured = fetched.reshape(width_all, PATCH, PATCH)[slot_of]
    grads = task_grad(patches, measured, probe)
    grads = grads * live

    def add_patch(index, total):
        start_y = offsets[index, 0] + half
        start_x = offsets[index, 1] + half
        current = lax.dynamic_slice(total, (zero, start_y, start_x), (2, PATCH, PATCH))
        return lax.dynamic_update_slice(total, current + grads[index], (zero, start_y, start_x))

    summed = lax.fori_loop(
        0, TASKS, add_patch, jnp.zeros((2, tile + 2 * half, tile + 2 * half), jnp.float32)
    )
    side_cols = jnp.zeros((2, tile + 2 * half, tile), jnp.float32)
    side_cols = side_cols.at[:, :, :half].set(summed[:, :, :half])
    side_cols = side_cols.at[:, :, tile - half :].set(summed[:, :, tile + half :])
    beside = extended_2(side_cols, (("gx", 2),), half)
    middle = summed[:, :, half : half + tile]
    middle = middle.at[:, :, :half].add(beside[:, :, :half])
    middle = middle.at[:, :, tile - half :].add(beside[:, :, tile + half :])
    side_rows = jnp.zeros((2, tile, tile), jnp.float32)
    side_rows = side_rows.at[:, :half, :].set(middle[:, :half, :])
    side_rows = side_rows.at[:, tile - half :, :].set(middle[:, tile + half :, :])
    above = extended_2(side_rows, (("gy", 1),), half)
    gradient = middle[:, half : half + tile, :]
    gradient = gradient.at[:, :half, :].add(above[:, :half, :])
    gradient = gradient.at[:, tile - half :, :].add(above[:, tile + half :, :])
    return object_field - step_size * (gradient + ridge * object_field)


def solution(mesh):
    in_specs = (
        P(None, "gy", "gx"),
        P(),
        P("gy", "gx", None, None, None, None),
        P("gy", "gx", None, None),
        P("gy", "gx", None, None),
        P("gy", "gx"),
    )
    out_specs = P(None, "gy", "gx")
    return jax.shard_map(
        per_device, mesh=mesh, in_specs=in_specs, out_specs=out_specs, check_vma=False
    )
```

profile of v0, /device:TPU:17, one launch (start us, length us, event | category | flops | bytes accessed | tf_op | source)
XLA Modules:
  0.0 886.2 jit_solution(6971625636656649953)
XLA Ops:
  2.3 3.1 collective-permute-start
  5.4 5.8 all-to-all-start
  11.2 3.2 collective-permute-start.1
  15.3 34.7 %collective-permute-done = f32[2,512,128]{2,1,0:T(8,128)} collective-permute-done((f32[2,512,128]{2,1,0:T(8,128)}, f32[2,512,128]{2,1,0:T(8,128)}, u32[]{:S(2)}, u32[]{:S(2)}) %collective-permute-start) | collective-permute-done | bytes 524320 | tf_op jit(solution)/shard_map/ppermute | solution.py:19
  51.2 105.5 %collective-permute-done.1 = f32[2,512,128]{2,1,0:T(8,128)} collective-permute-done((f32[2,512,128]{2,1,0:T(8,128)}, f32[2,512,128]{2,1,0:T(8,128)}, u32[]{:S(2)}, u32[]{:S(2)}) %collective-permute-start.1) | collective-permute-done | bytes 524320 | tf_op jit(solution)/shard_map/ppermute | solution.py:22
  160.7 4.8 collective-permute-start.2
  167.9 6.9 collective-permute-done.2
  174.8 4.3 collective-permute-done.3
  179.1 4.3 pad_maximum_fusion
  183.4 103.5 %while.26 = (s32[]{:T(128)}, f32[2,768,768]{2,1,0:T(8,128)}, s32[24,3]{0,1:T(4,128)S(1)}, f32[24,2,256,256]{2,3,0,1:T(8,128)}, s32[]{:T(128)}) while((s32[]{:T(128)}, f32[2,768,768]{2,1,0:T(8,128)}, s32[24,3]{0,1:T(4,128)S(1)}, f32[24,2,256,256]{2,3,0,1:T(8,128)}, s32[]{:T(128)}) %tuple.99), condition=%wide.while_cond.8, body=%wide.while_body.8.sunk | while | flops 2 | bytes 3145853 | solution.py:89
  188.3 2.6 dynamic-slice_bitcast_fusion.2
  192.6 2.6 dynamic-slice_bitcast_fusion.2
  205.5 2.6 dynamic-slice_bitcast_fusion.2
  209.8 2.6 dynamic-slice_bitcast_fusion.2
  214.2 2.6 dynamic-slice_bitcast_fusion.2
  227.1 2.6 dynamic-slice_bitcast_fusion.2
  235.7 2.6 dynamic-slice_bitcast_fusion.2
  286.8 10.9 %broadcast_multiply_fusion = f32[24,2,256,256]{2,3,0,1:T(8,128)} fusion(f32[24,2,256,256]{2,3,0,1:T(8,128)} %get-tuple-element.233, f32[24]{0:T(128)S(1)} %compare_convert_fusion), kind=kLoop, calls=%fused_computation.34 | loop fusion | flops 3145728 | bytes 25165920 | tf_op jit(solution)/shard_map/mul | solution.py:94
  297.8 16.0 %fusion.27 = f32[24,256,256]{2,1,0:T(8,128)S(1)} fusion(f32[24,2,256,256]{2,3,0,1:T(8,128)} %broadcast_multiply_fusion, f32[256,256]{0,1:T(8,128)S(1)} %copy.42, f32[256,256]{0,1:T(8,128)S(1)} %copy.40), kind=kOutput, calls=%fused_computation.44 | convolution fusion | flops 4837605376 | bytes 19398656 | tf_op jit(solution)/shard_map/bij,jk->bik/dot_general | solution.py:38
  313.8 11.7 %fusion.26 = f32[24,256,256]{2,1,0:T(8,128)S(1)} fusion(f32[24,2,256,256]{2,3,0,1:T(8,128)S(1)} %copy-done.4, f32[256,256]{0,1:T(8,128)S(1)} %copy.42, f32[256,256]{0,1:T(8,128)S(1)} %copy.40), kind=kOutput, calls=%fused_computation.43 | convolution fusion | flops 4837539840 | bytes 19398656 | tf_op jit(solution)/shard_map/bij,jk->bik/dot_general | solution.py:37
  325.6 22.1 %subtract_subtract_fusion.1 = f32[24,256,256]{2,1,0:T(8,128)} fusion(f32[24,256,256]{2,1,0:T(8,128)S(1)} %fusion.27, f32[24,256,256]{2,1,0:T(8,128)S(1)} %fusion.26, f32[24,2,256,256]{2,3,0,1:T(8,128)} %broadcast_multiply_fusion, f32[256,256]{0,1:T(8,128)S(1)} %copy.42, f32[256,256]{0,1:T(8,128)S(1)} %copy.40), kind=kOutput, calls=%fused_computation.29 | convolution fusion | flops 4847173632 | bytes 31981568 | tf_op jit(solution)/shard_map/bij,jk->bik/dot_general | solution.py:39
  347.7 15.5 %fusion.42 = f32[24,256,256]{2,1,0:T(8,128)} fusion(f32[24,256,256]{2,1,0:T(8,128)} %subtract_subtract_fusion.1), kind=kOutput, calls=%fused_computation.68 | convolution fusion | flops 4832886784 | bytes 12582912 | tf_op jit(solution)/shard_map/ij,bjk->bik/dot_general | solution.py:46
  363.2 13.7 %fusion.16 = f32[24,256,256]{2,1,0:T(8,128)} fusion(f32[24,256,256]{2,1,0:T(8,128)S(1)} %fusion.26, f32[24,256,256]{2,1,0:T(8,128)S(1)} %fusion.27), kind=kOutput, calls=%fused_computation.40 | convolution fusion | flops 4834394112 | bytes 18874368 | tf_op jit(solution)/shard_map/ij,bjk->bik/dot_general | solution.py:45
  376.9 6.3 gather_fusion
  383.2 6.6 copy.49
  389.8 34.1 %fusion.7 = (f32[24,256,256]{1,2,0:T(8,128)}, f32[24,256,256]{1,2,0:T(8,128)}) fusion(f32[24,256,256]{1,2,0:T(8,128)} %copy.49, f32[24,256,256]{2,1,0:T(8,128)} %fusion.42, f32[24,256,256]{2,1,0:T(8,128)} %fusion.16, f32[24,256,256]{2,1,0:T(8,128)} %subtract_subtract_fusion.1, f32[24,256,256]{2,1,0:T(8,128)} %copy-done.1, f32[24,256,256]{2,1,0:T(8,128)} %copy-done), kind=kOutput, calls=%fused_computation.26 | convolution fusion | flops 4850319360 | bytes 50331648 | tf_op jit(solution)/shard_map/ij,bjk->bik/dot_general | solution.py:47
  423.9 14.8 %fusion.46 = f32[24,256,256]{2,1,0:T(8,128)S(1)} fusion(f32[24,256,256]{1,2,0:T(8,128)} %get-tuple-element.266), kind=kOutput, calls=%fused_computation.72 | convolution fusion | flops 4832821248 | bytes 12582912 | tf_op jit(solution)/shard_map/bij,jk->bik/dot_general | solution.py:37
  438.8 11.7 %fusion.38 = f32[24,256,256]{2,1,0:T(8,128)S(1)} fusion(f32[24,256,256]{1,2,0:T(8,128)S(1)} %copy-done.5), kind=kOutput, calls=%fused_computation.64 | convolution fusion | flops 4832952320 | bytes 12582912 | tf_op jit(solution)/shard_map/bij,jk->bik/dot_general | solution.py:38
  450.6 19.5 %subtract_subtract_fusion = f32[24,256,256]{2,1,0:T(8,128)} fusion(f32[24,256,256]{2,1,0:T(8,128)S(1)} %fusion.38, f32[24,256,256]{2,1,0:T(8,128)S(1)} %fusion.46, f32[24,256,256]{1,2,0:T(8,128)S(1)} %bitcast.157, f32[24,256,256]{1,2,0:T(8,128)} %get-tuple-element.267), kind=kOutput, calls=%fused_computation.21 | convolution fusion | flops 4837801984 | bytes 31457280 | tf_op jit(solution)/shard_map/bij,jk->bik/dot_general | solution.py:39
  470.1 13.8 %fusion.13 = f32[24,256,256]{2,1,0:T(8,128)} fusion(f32[24,256,256]{2,1,0:T(8,128)S(1)} %fusion.46, f32[24,256,256]{2,1,0:T(8,128)S(1)} %fusion.38), kind=kOutput, calls=%fused_computation.37 | convolution fusion | flops 4834394112 | bytes 18874368 | tf_op jit(solution)/shard_map/ij,bjk->bik/dot_general | solution.py:45
  483.9 14.7 %fusion.36 = f32[24,256,256]{2,1,0:T(8,128)} fusion(f32[24,256,256]{2,1,0:T(8,128)S(1)} %copy-done.6), kind=kOutput, calls=%fused_computation.62 | convolution fusion | flops 4832952320 | bytes 12582912 | tf_op jit(solution)/shard_map/ij,bjk->bik/dot_general | solution.py:46
  498.6 27.8 %add_bitcast_fusion = (f32[24,1,256,256]{2,3,0,1:T(8,128)}, f32[24,1,256,256]{2,3,0,1:T(8,128)}) fusion(f32[256,256]{0,1:T(8,128)S(1)} %copy.42, f32[256,256]{0,1:T(8,128)S(1)} %copy.40, f32[24,256,256]{2,1,0:T(8,128)} %fusion.36, f32[24,256,256]{2,1,0:T(8,128)} %fusion.13, f32[24,256,256]{2,1,0:T(8,128)} %subtract_subtract_fusion, ...), kind=kOutput, calls=%fused_computation.18 | convolution fusion | flops 4850384896 | bytes 44564480 | tf_op jit(solution)/shard_map/ij,bjk->bik/dot_general | solution.py:47
  526.4 11.0 %maximum_multiply_fusion = f32[24,2,256,256]{2,3,0,1:T(8,128)} fusion(f32[24,1,256,256]{2,3,0,1:T(8,128)} %get-tuple-element.269, f32[24,1,256,256]{2,3,0,1:T(8,128)} %get-tuple-element.268, f32[24]{0:T(128)S(1)} %compare_convert_fusion), kind=kLoop, calls=%fused_computation.8 | loop fusion | flops 6291456 | bytes 25165920 | tf_op jit(solution)/shard_map/mul | solution.py:98
  539.8 299.4 %while.25 = (s32[]{:T(128)}, f32[2,768,768]{2,1,0:T(8,128)}, s32[24,2]{0,1:T(2,128)S(1)}, f32[24,2,256,256]{2,3,0,1:T(8,128)}, s32[]{:T(128)}, /*index=5*/s32[1,1]{0,1:T(1,128)}, s32[]{:T(128)}, s32[1,1]{0,1:T(1,128)}) while((s32[]{:T(128)}, f32[2,768,768]{2,1,0:T(8,128)}, s32[24,2]{0,1:T(2,128)S(1)}, f32[24,2,256,256]{2,3,0,1:T(8,128)}, ...), condition=%wide.region_2.3_spmd, body=%wide.region_1.2_spmd.sunk | while | flops 131082 | bytes 4718813 | solution.py:106
  545.6 6.8 dynamic_update_slice.12
  558.2 6.8 dynamic_update_slice.12
  570.9 6.8 dynamic_update_slice.12
  583.5 6.3 dynamic_update_slice.12
  595.6 6.8 dynamic_update_slice.12
  608.3 6.7 dynamic_update_slice.12
  620.8 6.8 dynamic_update_slice.12
  633.5 6.5 dynamic_update_slice.12
  645.8 6.7 dynamic_update_slice.12
  658.4 6.2 dynamic_update_slice.12
  670.4 6.8 dynamic_update_slice.12
  683.1 6.4 dynamic_update_slice.12
  695.3 6.6 dynamic_update_slice.12
  707.7 6.6 dynamic_update_slice.12
  720.1 6.5 dynamic_update_slice.12
  732.5 6.6 dynamic_update_slice.12
  745.0 6.5 dynamic_update_slice.12
  757.3 6.7 dynamic_update_slice.12
  769.9 6.8 dynamic_update_slice.12
  782.6 6.2 dynamic_update_slice.12
  794.6 6.8 dynamic_update_slice.12
  807.2 6.7 dynamic_update_slice.12
  819.8 6.8 dynamic_update_slice.12
  832.4 6.8 dynamic_update_slice.12
  842.3 3.6 fusion.121
  846.0 4.3 collective-permute-start.5
  850.3 3.7 collective-permute-done.4
  855.3 15.0 %collective-permute-done.5 = f32[2,768,128]{2,1,0:T(8,128)S(1)} collective-permute-done((f32[2,768,128]{2,1,0:T(8,128)S(1)}, f32[2,768,128]{2,1,0:T(8,128)S(1)}, u32[]{:S(2)}, u32[]{:S(2)}) %collective-permute-start.5) | collective-permute-done | bytes 786464 | tf_op jit(solution)/shard_map/ppermute | solution.py:22
  875.7 3.0 collective-permute-done.6
  878.8 4.9 collective-permute-done.7
  (274 shorter events, 187.2 us)
Async XLA Ops:
  2.3 47.7 %collective-permute-start = (f32[2,512,128]{2,1,0:T(8,128)}, f32[2,512,128]{2,1,0:T(8,128)}, u32[]{:S(2)}, u32[]{:S(2)}) collective-permute-start(f32[2,512,128]{2,1,0:T(8,128)} %get-tuple-element.277), channel_id=1, source_target_pairs={{0,4},{4,8},{8,12},{12,16},{16,20},{20,24},{24,28},{1,5},{5,9},{9,... | collective-permute-start | bytes 1572872 | tf_op jit(solution)/shard_map/ppermute | solution.py:19
  5.4 9.0 %copy-start.10 = (f32[2,256,256]{2,1,0:T(8,128)S(1)}, f32[2,256,256]{2,1,0:T(8,128)}, u32[]{:S(2)}) copy-start(f32[2,256,256]{2,1,0:T(8,128)} %param.25) | copy-start | bytes 1572868
  5.4 45.6 %copy-start.7 = (f32[2,512,512]{2,1,0:T(8,128)S(1)}, f32[2,512,512]{2,1,0:T(8,128)}, u32[]{:S(2)}) copy-start(f32[2,512,512]{2,1,0:T(8,128)} %param.24) | copy-start | bytes 6291460
  5.4 371.4 %all-to-all-start = ((f32[8,3,256,256]{3,2,1,0:T(8,128)}), f32[8,3,256,256]{3,2,1,0:T(8,128)}, u32[]{:S(2)}, u32[]{:S(2)}) async-start(f32[8,3,256,256]{3,2,1,0:T(8,128)} %bitcast.158), calls=%async_computation | async-start | bytes 12582912 | tf_op jit(solution)/shard_map/all_to_all | solution.py:95
  11.2 156.4 %copy-start.11 = (s32[1,1,24,2]{2,3,1,0:T(2,128)S(1)}, s32[1,1,24,2]{2,3,1,0:T(2,128)}, u32[]{:S(2)}) copy-start(s32[1,1,24,2]{2,3,1,0:T(2,128)} %param.27) | copy-start | bytes 580
  11.2 156.4 %copy-start.13 = (s32[1,1,24,1]{2,3,1,0:T(1,128)S(1)}, s32[1,1,24,1]{2,3,1,0:T(1,128)}, u32[]{:S(2)}) copy-start(s32[1,1,24,1]{2,3,1,0:T(1,128)} %param.28) | copy-start | bytes 292
  11.2 145.5 %collective-permute-start.1 = (f32[2,512,128]{2,1,0:T(8,128)}, f32[2,512,128]{2,1,0:T(8,128)}, u32[]{:S(2)}, u32[]{:S(2)}) collective-permute-start(f32[2,512,128]{2,1,0:T(8,128)} %get-tuple-element.276), channel_id=1, source_target_pairs={{4,0},{8,4},{12,8},{16,12},{20,16},{24,20},{28,24},{5,1},{9,5},{13... | collective-permute-start | bytes 1572872 | tf_op jit(solution)/shard_map/ppermute | solution.py:22
  157.8 1.6 copy-start.9
  160.7 14.0 %collective-permute-start.2 = (f32[2,128,768]{2,1,0:T(8,128)}, f32[2,128,768]{2,1,0:T(8,128)S(1)}, u32[]{:S(2)}, u32[]{:S(2)}) collective-permute-start(f32[2,128,768]{2,1,0:T(8,128)} %get-tuple-element.274), channel_id=1, source_target_pairs={{0,1},{1,2},{2,3},{4,5},{5,6},{6,7},{8,9},{9,10},{10,11},{12,13},{... | collective-permute-start | bytes 2359304 | tf_op jit(solution)/shard_map/ppermute | solution.py:19
  165.5 13.5 %collective-permute-start.3 = (f32[2,128,768]{2,1,0:T(8,128)}, f32[2,128,768]{2,1,0:T(8,128)S(1)}, u32[]{:S(2)}, u32[]{:S(2)}) collective-permute-start(f32[2,128,768]{2,1,0:T(8,128)} %get-tuple-element.275), channel_id=1, source_target_pairs={{1,0},{2,1},{3,2},{5,4},{6,5},{7,6},{9,8},{10,9},{11,10},{13,12},{... | collective-permute-start | bytes 2359304 | tf_op jit(solution)/shard_map/ppermute | solution.py:22
  297.8 16.0 %copy-start.4 = (f32[24,2,256,256]{2,3,0,1:T(8,128)S(1)}, f32[24,2,256,256]{2,3,0,1:T(8,128)}, u32[]{:S(2)}) copy-start(f32[24,2,256,256]{2,3,0,1:T(8,128)} %broadcast_multiply_fusion) | copy-start | bytes 37748740
  313.8 49.4 %copy-start = (f32[24,256,256]{2,1,0:T(8,128)}, f32[24,256,256]{2,1,0:T(8,128)S(1)}, u32[]{:S(2)}) copy-start(f32[24,256,256]{2,1,0:T(8,128)S(1)} %fusion.27) | copy-start | bytes 18874372
  325.5 37.7 %copy-start.1 = (f32[24,256,256]{2,1,0:T(8,128)}, f32[24,256,256]{2,1,0:T(8,128)S(1)}, u32[]{:S(2)}) copy-start(f32[24,256,256]{2,1,0:T(8,128)S(1)} %fusion.26) | copy-start | bytes 18874372
  423.9 14.9 %copy-start.5 = (f32[24,256,256]{1,2,0:T(8,128)S(1)}, f32[24,256,256]{1,2,0:T(8,128)}, u32[]{:S(2)}) copy-start(f32[24,256,256]{1,2,0:T(8,128)} %get-tuple-element.267) | copy-start | bytes 18874372
  423.9 26.6 %slice-start = ((s8[6291456]{0:T(1024)(128)(4,1)}), s8[4194304]{0:T(1024)(128)(4,1)S(1)}, s32[]{:S(2)}) async-start(s8[6291456]{0:T(1024)(128)(4,1)} %bitcast.156), calls=%async_computation.1 | async-start | bytes 8388608
  438.8 31.3 %copy-start.2 = (f32[24,256,256]{2,1,0:T(8,128)}, f32[24,256,256]{2,1,0:T(8,128)S(1)}, u32[]{:S(2)}) copy-start(f32[24,256,256]{2,1,0:T(8,128)S(1)} %fusion.46) | copy-start | bytes 18874372
  438.8 11.8 %slice-start.1 = ((s8[6291456]{0:T(1024)(128)(4,1)}), s8[2097152]{0:T(1024)(128)(4,1)S(1)}, s32[]{:S(2)}) async-start(s8[6291456]{0:T(1024)(128)(4,1)} %bitcast.156), calls=%async_computation.2 | async-start | bytes 4194304
  450.6 19.5 %copy-start.3 = (f32[24,256,256]{2,1,0:T(8,128)}, f32[24,256,256]{2,1,0:T(8,128)S(1)}, u32[]{:S(2)}) copy-start(f32[24,256,256]{2,1,0:T(8,128)S(1)} %fusion.38) | copy-start | bytes 18874372
  470.1 13.8 %copy-start.6 = (f32[24,256,256]{2,1,0:T(8,128)S(1)}, f32[24,256,256]{2,1,0:T(8,128)}, u32[]{:S(2)}) copy-start(f32[24,256,256]{2,1,0:T(8,128)} %subtract_subtract_fusion) | copy-start | bytes 18874372
  840.4 5.6 copy-start.12
  840.4 13.7 %collective-permute-start.4 = (f32[2,768,128]{2,1,0:T(8,128)S(1)}, f32[2,768,128]{2,1,0:T(8,128)S(1)}, u32[]{:S(2)}, u32[]{:S(2)}) collective-permute-start(f32[2,768,128]{2,1,0:T(8,128)S(1)} %slice.254), channel_id=1, source_target_pairs={{0,4},{4,8},{8,12},{12,16},{16,20},{20,24},{24,28},{1,5},{5,9},{9,... | collective-permute-start | bytes 2359304 | tf_op jit(solution)/shard_map/ppermute | solution.py:19
  846.0 24.3 %collective-permute-start.5 = (f32[2,768,128]{2,1,0:T(8,128)S(1)}, f32[2,768,128]{2,1,0:T(8,128)S(1)}, u32[]{:S(2)}, u32[]{:S(2)}) collective-permute-start(f32[2,768,128]{2,1,0:T(8,128)S(1)} %slice_select_fusion), channel_id=1, source_target_pairs={{4,0},{8,4},{12,8},{16,12},{20,16},{24,20},{28,24},{5,1},{9,5},{13... | collective-permute-start | bytes 2359304 | tf_op jit(solution)/shard_map/ppermute | solution.py:22
  870.6 13.4 %copy-start.8 = (f32[2,512,512]{2,1,0:T(8,128)S(1)}, f32[2,512,512]{2,1,0:T(8,128)}, u32[]{:S(2)}) copy-start(f32[2,512,512]{2,1,0:T(8,128)} %param.24) | copy-start | bytes 6291460
  870.6 8.2 collective-permute-start.6
  873.3 10.5 %collective-permute-start.7 = (f32[2,128,512]{2,1,0:T(8,128)S(1)}, f32[2,128,512]{2,1,0:T(8,128)S(1)}, u32[]{:S(2)}, u32[]{:S(2)}) collective-permute-start(f32[2,128,512]{2,1,0:T(8,128)S(1)} %slice_select_fusion.1), channel_id=1, source_target_pairs={{1,0},{2,1},{3,2},{5,4},{6,5},{7,6},{9,8},{10,9},{11,10},{13,12},{... | collective-permute-start | bytes 1572872 | tf_op jit(solution)/shard_map/ppermute | solution.py:22
where the time goes:
time: 903 us; the launch traced here: 886 us
  local copies, waits for them, and re-layouts  336 us (37%)
  matrix products  216 us (24%)
  waiting for transfers between devices  178 us (20%)
  other arithmetic  63 us (7%)
  loops' own time  62.3 us (7%)
  starting transfers between devices  29.5 us (3%)
    dynamic_update_slice x24, local copies, waits for them, and re-layouts, add_patch(): lax.dynamic_update_slice(total, current + grads[index], (zero, start_y, s...  159 us
    ppermute x4, waiting for transfers between devices, extended_2(): lax.ppermute(lax.slice_in_dim(block, 0, width, axis=dim), axis, backward)  130 us
    gather x120, local copies, waits for them, and re-layouts  103 us
    another operation x1, loops' own time, per_device(): lax.fori_loop(0, TASKS, add_patch, jnp.zeros((2, tile + 2 * half, tile +...  62.1 us
    dot_general x2, matrix products, left_mul(): jnp.einsum('ij,bjk->bik', table_re + table_im, real_in + imag_in, precisi...  61.9 us
    ppermute x4, waiting for transfers between devices, extended_2(): lax.ppermute(lax.slice_in_dim(block, block.shape[dim] - width, None, axis...  48.3 us
    dot_general x2, matrix products, right_mul(): jnp.einsum('bij,jk->bik', real_in + imag_in, table_re + table_im, precisi...  41.6 us
    add x24, other arithmetic, add_patch(): current + grads[index]  32.9 us
  transfers between devices with their start and end apart: 9, of which 8 were waited for; matrix products, arithmetic and copies ran while one was open for 23% of the time, Pallas kernels for 0%

commit v1 on v0

v1 whole, which is shorter than its diff:
```python
import functools

import jax
import jax.numpy as jnp
import numpy as np
from jax import lax
from jax.experimental import pallas as pl
from jax.experimental.pallas import tpu as pltpu
from jax.sharding import PartitionSpec as P

step_size = 0.1
ridge = 0.5
f32 = jnp.float32
bf16 = jnp.bfloat16


def split_np(table):
    hi = table.astype(jnp.bfloat16)
    lo = (table - hi.astype(np.float64)).astype(jnp.bfloat16)
    return hi, lo


def dft_tables(length):
    half = length // 2
    n = np.arange(half)[:, None]
    rights, lefts = [], []
    for parity in (0, 1):
        k = 2 * np.arange(half)[None, :] + parity
        angle = -2.0 * np.pi / length * ((n * k) % length)
        re, im = np.cos(angle) * length**-0.5, np.sin(angle) * length**-0.5
        right = np.block([[re, im], [-im, re]])
        hi, lo = split_np(right)
        rights.append(np.concatenate([hi, hi, lo], axis=0))
        hi, lo = split_np(right.T)
        lefts.append(np.concatenate([hi, hi, lo], axis=0))
    right = np.stack(rights)
    right_t = np.stack(lefts)
    left = np.stack([t.T for t in rights])
    left_t = np.stack([t.T for t in lefts])
    perm = np.zeros((length, length))
    order = np.concatenate([np.arange(0, length, 2), np.arange(1, length, 2)])
    perm[order, np.arange(length)] = 1.0
    perm = perm.astype(jnp.bfloat16)
    return right, right_t, left, left_t, np.concatenate([perm, perm], axis=0)


def halves(x):
    hi = x.astype(bf16)
    return hi, (x - hi.astype(f32)).astype(bf16)


def mul_right(x, table):
    hi, lo = halves(x)
    return jnp.dot(jnp.concatenate([hi, lo, hi], axis=1), table, preferred_element_type=f32)


def mul_left(table, x):
    hi, lo = halves(x)
    return jnp.dot(table, jnp.concatenate([hi, lo, hi], axis=0), preferred_element_type=f32)


def masks(a_y, a_x, size):
    rows = lax.broadcasted_iota(jnp.int32, (size, size), 0) >= a_y
    cols = lax.broadcasted_iota(jnp.int32, (size, size), 1) >= a_x
    return rows, cols


def rolled_probe(probe_ref, a_y, a_x):
    return [
        pltpu.roll(pltpu.roll(probe_ref[part], a_x, 1), a_y, 0) for part in range(2)
    ]


def place(info_ref, index, size, blocks):
    start_y, start_x = info_ref[0, index], info_ref[1, index]
    k_y, k_x = start_y // size, start_x // size
    ys = (k_y, jnp.minimum(k_y + 1, blocks - 1))
    xs = (k_x, jnp.minimum(k_x + 1, blocks - 1))
    return ys, xs, start_y - k_y * size, start_x - k_x * size


def window(ref, part, y, x, size):
    return ref.at[
        part, pl.ds(pl.multiple_of(y * size, size), size), pl.ds(pl.multiple_of(x * size, size), size)
    ]


def forward_kernel(blocks, info_ref, field_ref, probe_ref, right_ref, left_ref, far_ref):
    size = probe_ref.shape[1]
    half = size // 2
    index = pl.program_id(0)

    @pl.when(info_ref[2, index] > 0)
    def _():
        ys, xs, a_y, a_x = place(info_ref, index, size, blocks)
        rows, cols = masks(a_y, a_x, size)
        obj = []
        for part in range(2):
            first = jnp.where(cols, window(field_ref, part, ys[0], xs[0], size)[...],
                              window(field_ref, part, ys[0], xs[1], size)[...])
            second = jnp.where(cols, window(field_ref, part, ys[1], xs[0], size)[...],
                               window(field_ref, part, ys[1], xs[1], size)[...])
            obj.append(jnp.where(rows, first, second))
        p_re, p_im = rolled_probe(probe_ref, a_y, a_x)
        re = p_re * obj[0] - p_im * obj[1]
        im = p_re * obj[1] + p_im * obj[0]
        even = mul_right(
            jnp.concatenate([re[:, :half] + re[:, half:], im[:, :half] + im[:, half:]], axis=1), right_ref[0]
        )
        odd = mul_right(
            jnp.concatenate([re[:, :half] - re[:, half:], im[:, :half] - im[:, half:]], axis=1), right_ref[1]
        )
        re = jnp.concatenate([even[:, :half], odd[:, :half]], axis=1)
        im = jnp.concatenate([even[:, half:], odd[:, half:]], axis=1)
        far_ref[0, 0] = mul_left(
            left_ref[0], jnp.concatenate([re[:half] + re[half:], im[:half] + im[half:]], axis=0)
        )
        far_ref[0, 1] = mul_left(
            left_ref[1], jnp.concatenate([re[:half] - re[half:], im[:half] - im[half:]], axis=0)
        )


def backward_kernel(
    blocks, info_ref, far_ref, frame_ref, probe_ref, right_ref, left_ref, perm_ref, grad_ref, sorted_ref
):
    size = probe_ref.shape[1]
    half = size // 2
    index = pl.program_id(0)

    @pl.when(index == 0)
    def _():
        grad_ref[...] = jnp.zeros_like(grad_ref)

    @pl.when(info_ref[2, index] > 0)
    def _():
        ys, xs, a_y, a_x = place(info_ref, index, size, blocks)
        hi, lo = halves(frame_ref[0])
        frame = jnp.dot(jnp.concatenate([hi, lo], axis=1), perm_ref[...], preferred_element_type=f32)
        sorted_ref[0] = frame[:, :half]
        sorted_ref[1] = frame[:, half:]
        back = []
        for parity in range(2):
            frame = jnp.concatenate(
                [sorted_ref[col, pl.ds(parity, half, stride=2), :] for col in range(2)], axis=1
            )
            far = far_ref[0, parity]
            re, im = far[:half], far[half:]
            weight = re * re + im * im - frame
            back.append(mul_left(left_ref[parity], jnp.concatenate([weight * re, weight * im], axis=0)))
        top, bottom = back[0] + back[1], back[0] - back[1]
        re = jnp.concatenate([top[:half], bottom[:half]], axis=0)
        im = jnp.concatenate([top[half:], bottom[half:]], axis=0)
        even = mul_right(jnp.concatenate([re[:, :half], im[:, :half]], axis=1), right_ref[0])
        odd = mul_right(jnp.concatenate([re[:, half:], im[:, half:]], axis=1), right_ref[1])
        low, high = even + odd, even - odd
        re = jnp.concatenate([low[:, :half], high[:, :half]], axis=1)
        im = jnp.concatenate([low[:, half:], high[:, half:]], axis=1)
        p_re, p_im = rolled_probe(probe_ref, a_y, a_x)
        grads = (p_re * re + p_im * im, p_re * im - p_im * re)
        rows, cols = masks(a_y, a_x, size)
        for part in range(2):
            for row in range(2):
                for col in range(2):
                    keep = jnp.logical_and(rows == (row == 0), cols == (col == 0))
                    where = window(grad_ref, part, ys[row], xs[col], size)
                    where[...] += jnp.where(keep, grads[part], 0.0)


def whole(shape):
    return pl.BlockSpec(shape, lambda i, *refs: (0,) * len(shape))


def run_forward(info, field, probe, right, left):
    count, size = info.shape[1], probe.shape[1]
    return pl.pallas_call(
        functools.partial(forward_kernel, field.shape[1] // size),
        out_shape=jax.ShapeDtypeStruct((count, 2, size, size), f32),
        grid_spec=pltpu.PrefetchScalarGridSpec(
            num_scalar_prefetch=1,
            grid=(count,),
            in_specs=[whole(field.shape), whole(probe.shape), whole(right.shape), whole(left.shape)],
            out_specs=pl.BlockSpec((1, 2, size, size), lambda i, *refs: (i, 0, 0, 0)),
        ),
        compiler_params=pltpu.CompilerParams(vmem_limit_bytes=40 << 20),
        cost_estimate=pl.CostEstimate(
            flops=count * 24 * size**3, bytes_accessed=4 * (field.size + count * 2 * size**2), transcendentals=0
        ),
        name="forward",
    )(info, field, probe, right, left)


def run_backward(info, far, frames, probe, right, left, perm, extent):
    count, size = info.shape[1], probe.shape[1]
    return pl.pallas_call(
        functools.partial(backward_kernel, extent // size),
        out_shape=jax.ShapeDtypeStruct((2, extent, extent), f32),
        grid_spec=pltpu.PrefetchScalarGridSpec(
            num_scalar_prefetch=1,
            grid=(count,),
            in_specs=[
                pl.BlockSpec((1, 2, size, size), lambda i, info: (i, 0, 0, 0)),
                pl.BlockSpec((1, size, size), lambda i, info: (info[3, i], 0, 0)),
                whole(probe.shape), whole(right.shape), whole(left.shape), whole(perm.shape),
            ],
            out_specs=whole((2, extent, extent)),
            scratch_shapes=[pltpu.VMEM((2, size, size // 2), f32)],
        ),
        compiler_params=pltpu.CompilerParams(vmem_limit_bytes=40 << 20),
        cost_estimate=pl.CostEstimate(
            flops=count * 24 * size**3, bytes_accessed=4 * count * 3 * size**2, transcendentals=0
        ),
        name="backward",
    )(info, far, frames, probe, right, left, perm)


def from_sides(low_part, high_part, axis):
    count = lax.axis_size(axis)
    forward = [(i, i + 1) for i in range(count - 1)]
    backward = [(target, source) for source, target in forward]
    return lax.ppermute(high_part, axis, forward), lax.ppermute(low_part, axis, backward)


def per_device(object_field, probe, frames, positions, helpers, task_counts):
    tile, size = object_field.shape[1], probe.shape[1]
    half = size // 2
    extent = tile + 2 * half
    kept = frames[0, 0]
    sources, slots = kept.shape[:2]
    fetched = lax.all_to_all(kept, "gx", split_axis=0, concat_axis=0, tiled=True)
    fetched = fetched.reshape(sources * slots, size, size)

    before, after = from_sides(object_field[:, :, :half], object_field[:, :, tile - half :], "gx")
    field = jnp.concatenate([before, object_field, after], axis=2)
    before, after = from_sides(field[:, :half], field[:, tile - half :], "gy")
    field = jnp.concatenate([before, field, after], axis=1)

    offsets = positions[0, 0]
    tasks = offsets.shape[0]
    task_ids = jnp.arange(tasks, dtype=jnp.int32)
    valid = task_ids < task_counts[0, 0]
    helper_cols = helpers[0, 0, :, 0]
    same = helper_cols[:, None] == helper_cols[None, :]
    ranks = jnp.sum(jnp.logical_and(same, task_ids[None, :] < task_ids[:, None]), axis=1)
    info = jnp.stack(
        [offsets[:, 0] + half, offsets[:, 1] + half, valid.astype(jnp.int32), helper_cols * slots + ranks]
    ).astype(jnp.int32)

    right, right_t, left, left_t, perm = (jnp.asarray(t) for t in dft_tables(size))
    far = run_forward(info, field, probe, right, left)
    summed = run_backward(info, far, fetched, probe, right_t, left_t, perm, extent)

    before, after = from_sides(summed[:, :, :half], summed[:, :, tile + half :], "gx")
    middle = summed[:, :, half : half + tile]
    middle = middle.at[:, :, :half].add(before)
    middle = middle.at[:, :, tile - half :].add(after)
    before, after = from_sides(middle[:, :half], middle[:, tile + half :], "gy")
    gradient = middle[:, half : half + tile]
    gradient = gradient.at[:, :half].add(before)
    gradient = gradient.at[:, tile - half :].add(after)
    return object_field - step_size * (gradient + ridge * object_field)


def solution(mesh):
    in_specs = (
        P(None, "gy", "gx"),
        P(),
        P("gy", "gx", None, None, None, None),
        P("gy", "gx", None, None),
        P("gy", "gx", None, None),
        P("gy", "gx"),
    )
    out_specs = P(None, "gy", "gx")
    return jax.shard_map(
        per_device, mesh=mesh, in_specs=in_specs, out_specs=out_specs, check_vma=False
    )
```

time: 903 us -> 272 us (0.30); the launches traced: 886 us -> 271 us
  local copies, waits for them, and re-layouts: 336 us -> 1.23 us
  matrix products: 216 us -> 0 us
  loops' own time: 62.3 us -> 0 us
  Pallas kernels: 0 us -> 61.2 us
  other arithmetic: 63 us -> 2.87 us
    dot_general x12 -> x0, matrix products: 216 us -> none  [the longest x2 61.9 us: left_mul(): jnp.einsum('ij,bjk->bik', table_re + table_im, real_in + imag_in, precisi...]
    dynamic_update_slice x24 -> x0, local copies, waits for them, and re-layouts: 159 us -> none  [add_patch(): lax.dynamic_update_slice(total, current + grads[index], (zero, start_y, s...]
    gather x122 -> x0, local copies, waits for them, and re-layouts: 116 us -> none
    another operation x2 -> x0, loops' own time: 62.3 us -> none  [the longest x1 62.1 us: per_device(): lax.fori_loop(0, TASKS, add_patch, jnp.zeros((2, tile + 2 * half, tile +...]
    pallas_call x0 -> x2, Pallas kernels: none -> 61.2 us  [the longest x1 34.8 us: run_backward(): pl.pallas_call(functools.partial(backward_kernel, extent // size), out_sh...]
    dynamic_slice x72 -> x0, local copies, waits for them, and re-layouts: 45.3 us -> none  [the longest x48 30.8 us: add_patch(): grads[index]]
    add x24 -> x2, other arithmetic: 32.9 us -> 0.01 us  [the longest x1 0.01 us: per_device(): helper_cols * slots + ranks]
    mul x2 -> x0, other arithmetic: 21.9 us -> none  [the longest x1 11 us: per_device(): grads = grads * live]
  transfers between devices with their start and end apart: 9 -> 9, of which waited for: 8 -> 7; matrix products, arithmetic and copies ran while one was open for 23% -> 1% of each run, Pallas kernels for 0% -> 10%
where the time goes in v1:
time: 272 us; the launch traced here: 271 us
  waiting for transfers between devices  176 us (65%)
  Pallas kernels  61.2 us (22%)
  starting transfers between devices  28.5 us (10%)
  other arithmetic  2.87 us (1%)
    ppermute x4, waiting for transfers between devices, from_sides(): lax.ppermute(high_part, axis, forward)  159 us
    pallas_call x1, Pallas kernels, run_backward(): pl.pallas_call(functools.partial(backward_kernel, extent // size), out_sh...  34.8 us
    pallas_call x1, Pallas kernels, run_forward(): pl.pallas_call(functools.partial(forward_kernel, field.shape[1] // size),...  26.4 us
    ppermute x4, waiting for transfers between devices, from_sides(): lax.ppermute(low_part, axis, backward)  17 us
    ppermute x4, starting transfers between devices, from_sides(): lax.ppermute(high_part, axis, forward)  11.4 us
    ppermute x4, starting transfers between devices, from_sides(): lax.ppermute(low_part, axis, backward)  11.3 us
    all_to_all x1, starting transfers between devices, per_device(): lax.all_to_all(kept, 'gx', split_axis=0, concat_axis=0, tiled=True)  5.74 us
  transfers between devices with their start and end apart: 9, of which 7 were waited for; matrix products, arithmetic and copies ran while one was open for 1% of the time, Pallas kernels for 10%

profile of v1, /device:TPU:17, one launch (start us, length us, event | category | flops | bytes accessed | tf_op | source)
XLA Modules:
  0.0 271.2 jit_solution(17983141836082530297)
XLA Ops:
  0.0 0.0 copy-start.6
  0.0 5.7 %all-to-all-start = ((f32[8,3,256,256]{3,2,1,0:T(8,128)}), f32[8,3,256,256]{3,2,1,0:T(8,128)}, u32[]{:S(2)}, u32[]{:S(2)}) async-start(f32[8,3,256,256]{3,2,1,0:T(8,128)} %bitcast.14), calls=%async_computation | async-start | bytes 12582912 | tf_op jit(solution)/shard_map/all_to_all | solution.py:229
  5.7 0.0 copy-done.6
  5.7 0.1 fusion.8
  5.8 3.1 %collective-permute-start = (f32[2,512,128]{2,1,0:T(8,128)S(1)}, f32[2,512,128]{2,1,0:T(8,128)S(1)}, u32[]{:S(2)}, u32[]{:S(2)}) collective-permute-start(f32[2,512,128]{2,1,0:T(8,128)S(1)} %get-tuple-element.60), channel_id=1, source_target_pairs={{0,4},{4,8},{8,12},{12,16},{16,20},{20,24},{24,28},{1,5},{5,9},{9,... | collective-permute-start | bytes 1572872 | tf_op jit(solution)/shard_map/ppermute | solution.py:220
  8.9 3.1 %collective-permute-start.1 = (f32[2,512,128]{2,1,0:T(8,128)S(1)}, f32[2,512,128]{2,1,0:T(8,128)S(1)}, u32[]{:S(2)}, u32[]{:S(2)}) collective-permute-start(f32[2,512,128]{2,1,0:T(8,128)S(1)} %get-tuple-element.59), channel_id=1, source_target_pairs={{4,0},{8,4},{12,8},{16,12},{20,16},{24,20},{28,24},{5,1},{9,5},{13... | collective-permute-start | bytes 1572872 | tf_op jit(solution)/shard_map/ppermute | solution.py:220
  12.0 142.4 %collective-permute-done = f32[2,512,128]{2,1,0:T(8,128)S(1)} collective-permute-done((f32[2,512,128]{2,1,0:T(8,128)S(1)}, f32[2,512,128]{2,1,0:T(8,128)S(1)}, u32[]{:S(2)}, u32[]{:S(2)}) %collective-permute-start) | collective-permute-done | bytes 524320 | tf_op jit(solution)/shard_map/ppermute | solution.py:220
  154.4 0.2 constant_dynamic-update-slice_fusion.1
  154.6 0.0 copy-start.9
  154.6 0.0 copy-start.8
  154.6 0.0 collective-permute-done.1
  154.7 0.1 fusion.7
  154.8 3.5 %collective-permute-start.2 = (f32[2,128,768]{2,1,0:T(8,128)S(1)}, f32[2,128,768]{2,1,0:T(8,128)S(1)}, u32[]{:S(2)}, u32[]{:S(2)}) collective-permute-start(f32[2,128,768]{2,1,0:T(8,128)S(1)} %get-tuple-element.57), channel_id=1, source_target_pairs={{0,1},{1,2},{2,3},{4,5},{5,6},{6,7},{8,9},{9,10},{10,11},{12,13},{... | collective-permute-start | bytes 2359304 | tf_op jit(solution)/shard_map/ppermute | solution.py:220
  158.3 1.9 collective-permute-start.3
  160.9 0.0 copy-done.9
  160.9 0.2 convert_reduce_fusion
  161.1 0.0 copy-done.8
  161.1 0.0 copy-start
  161.2 0.0 copy-start.1
  161.2 0.0 copy-start.4
  161.2 6.0 %collective-permute-done.2 = f32[2,128,768]{2,1,0:T(8,128)S(1)} collective-permute-done((f32[2,128,768]{2,1,0:T(8,128)S(1)}, f32[2,128,768]{2,1,0:T(8,128)S(1)}, u32[]{:S(2)}, u32[]{:S(2)}) %collective-permute-start.2) | collective-permute-done | bytes 786464 | tf_op jit(solution)/shard_map/ppermute | solution.py:220
  167.2 4.4 %collective-permute-done.3 = f32[2,128,768]{2,1,0:T(8,128)S(1)} collective-permute-done((f32[2,128,768]{2,1,0:T(8,128)S(1)}, f32[2,128,768]{2,1,0:T(8,128)S(1)}, u32[]{:S(2)}, u32[]{:S(2)}) %collective-permute-start.3) | collective-permute-done | bytes 786464 | tf_op jit(solution)/shard_map/ppermute | solution.py:220
  171.6 0.3 pad_maximum_fusion.field_ref
  171.9 0.0 copy-done
  171.9 0.0 copy-done.1
  172.0 0.0 copy-done.4
  172.0 0.0 copy-start.2
  172.0 0.0 copy-start.3
  172.0 0.0 copy-start.5
  172.0 26.4 %forward.1.far_ref = f32[24,2,256,256]{3,2,1,0:T(8,128)} custom-call(s32[4,24]{1,0:T(4,128)S(1)} %pad_add_fusion.info_ref, f32[2,768,768]{2,1,0:T(8,128)S(1)} %pad_maximum_fusion.field_ref, f32[2,256,256]{2,1,0:T(8,128)S(1)} %copy-done, bf16[2,768,256]{2,1,0:T(8,128)(2,1)S(1)} %copy-done.4, bf16[2,256,768]{2,1,0:T(8,128)(2,1)S(1)} %copy-done.1), custom_call_target="tpu_custom_call" | custom-call | flops 9663676416 | bytes 17301504 | tf_op jit(solution)/shard_map/forward/pallas_call | solution.py:175
  198.4 0.0 all-to-all-done
  198.4 0.0 copy-done.2
  198.4 0.0 copy-done.3
  198.4 0.0 copy-done.5
  198.4 34.8 %backward.1 = f32[2,768,768]{2,1,0:T(8,128)S(1)} custom-call(s32[4,24]{1,0:T(4,128)S(1)} %pad_add_fusion.info_ref, f32[24,2,256,256]{3,2,1,0:T(8,128)} %forward.1.far_ref, f32[24,256,256]{2,1,0:T(8,128)} %bitcast.8.frame_ref, f32[2,256,256]{2,1,0:T(8,128)S(1)} %copy-done, bf16[2,768,256]{2,1,0:T(8,128)(2,1)S(1)} %copy-done.3, ...), custom_call_target="tpu_custom_call" | custom-call | flops 9663676416 | bytes 18874368 | tf_op jit(solution)/shard_map/backward/pallas_call | solution.py:194
  233.2 0.1 fusion.5
  233.3 1.9 collective-permute-start.4
  235.3 4.3 %collective-permute-start.5 = (f32[2,768,128]{2,1,0:T(8,128)S(1)}, f32[2,768,128]{2,1,0:T(8,128)S(1)}, u32[]{:S(2)}, u32[]{:S(2)}) collective-permute-start(f32[2,768,128]{2,1,0:T(8,128)S(1)} %get-tuple-element.53), channel_id=1, source_target_pairs={{4,0},{8,4},{12,8},{16,12},{20,16},{24,20},{28,24},{5,1},{9,5},{13... | collective-permute-start | bytes 2359304 | tf_op jit(solution)/shard_map/ppermute | solution.py:220
  239.5 0.4 slice.152
  239.9 7.1 %collective-permute-done.4 = f32[2,768,128]{2,1,0:T(8,128)S(1)} collective-permute-done((f32[2,768,128]{2,1,0:T(8,128)S(1)}, f32[2,768,128]{2,1,0:T(8,128)S(1)}, u32[]{:S(2)}, u32[]{:S(2)}) %collective-permute-start.4) | collective-permute-done | bytes 786464 | tf_op jit(solution)/shard_map/ppermute | solution.py:220
  247.1 0.1 fusion.1
  247.2 8.2 %collective-permute-done.5 = f32[2,768,128]{2,1,0:T(8,128)S(1)} collective-permute-done((f32[2,768,128]{2,1,0:T(8,128)S(1)}, f32[2,768,128]{2,1,0:T(8,128)S(1)}, u32[]{:S(2)}, u32[]{:S(2)}) %collective-permute-start.5) | collective-permute-done | bytes 786464 | tf_op jit(solution)/shard_map/ppermute | solution.py:220
  255.4 0.2 fusion
  255.6 0.1 fusion.6
  255.6 2.9 %collective-permute-start.6 = (f32[2,128,512]{2,1,0:T(8,128)S(1)}, f32[2,128,512]{2,1,0:T(8,128)S(1)}, u32[]{:S(2)}, u32[]{:S(2)}) collective-permute-start(f32[2,128,512]{2,1,0:T(8,128)S(1)} %get-tuple-element.56), channel_id=1, source_target_pairs={{0,1},{1,2},{2,3},{4,5},{5,6},{6,7},{8,9},{9,10},{10,11},{12,13},{... | collective-permute-start | bytes 1572872 | tf_op jit(solution)/shard_map/ppermute | solution.py:220
  258.6 0.0 copy-start.7
  258.6 2.1 collective-permute-start.7
  260.6 0.2 slice.157
  260.8 3.9 %collective-permute-done.6 = f32[2,128,512]{2,1,0:T(8,128)S(1)} collective-permute-done((f32[2,128,512]{2,1,0:T(8,128)S(1)}, f32[2,128,512]{2,1,0:T(8,128)S(1)}, u32[]{:S(2)}, u32[]{:S(2)}) %collective-permute-start.6) | collective-permute-done | bytes 524320 | tf_op jit(solution)/shard_map/ppermute | solution.py:220
  264.7 0.1 fusion.3
  264.7 4.5 %collective-permute-done.7 = f32[2,128,512]{2,1,0:T(8,128)S(1)} collective-permute-done((f32[2,128,512]{2,1,0:T(8,128)S(1)}, f32[2,128,512]{2,1,0:T(8,128)S(1)}, u32[]{:S(2)}, u32[]{:S(2)}) %collective-permute-start.7) | collective-permute-done | bytes 524320 | tf_op jit(solution)/shard_map/ppermute | solution.py:220
  269.2 0.1 fusion.2
  269.3 0.0 copy-done.7
  269.4 1.8 multiply_subtract_fusion
  (6 shorter events, 0.1 us)
Async XLA Ops:
  0.0 5.7 %copy-start.6 = (f32[2,512,512]{2,1,0:T(8,128)S(1)}, f32[2,512,512]{2,1,0:T(8,128)}, u32[]{:S(2)}) copy-start(f32[2,512,512]{2,1,0:T(8,128)} %param.19) | copy-start | bytes 6291460
  0.0 198.4 %all-to-all-start = ((f32[8,3,256,256]{3,2,1,0:T(8,128)}), f32[8,3,256,256]{3,2,1,0:T(8,128)}, u32[]{:S(2)}, u32[]{:S(2)}) async-start(f32[8,3,256,256]{3,2,1,0:T(8,128)} %bitcast.14), calls=%async_computation | async-start | bytes 12582912 | tf_op jit(solution)/shard_map/all_to_all | solution.py:229
  5.8 148.6 %collective-permute-start = (f32[2,512,128]{2,1,0:T(8,128)S(1)}, f32[2,512,128]{2,1,0:T(8,128)S(1)}, u32[]{:S(2)}, u32[]{:S(2)}) collective-permute-start(f32[2,512,128]{2,1,0:T(8,128)S(1)} %get-tuple-element.60), channel_id=1, source_target_pairs={{0,4},{4,8},{8,12},{12,16},{16,20},{20,24},{24,28},{1,5},{5,9},{9,... | collective-permute-start | bytes 1572872 | tf_op jit(solution)/shard_map/ppermute | solution.py:220
  8.9 145.7 %collective-permute-start.1 = (f32[2,512,128]{2,1,0:T(8,128)S(1)}, f32[2,512,128]{2,1,0:T(8,128)S(1)}, u32[]{:S(2)}, u32[]{:S(2)}) collective-permute-start(f32[2,512,128]{2,1,0:T(8,128)S(1)} %get-tuple-element.59), channel_id=1, source_target_pairs={{4,0},{8,4},{12,8},{16,12},{20,16},{24,20},{28,24},{5,1},{9,5},{13... | collective-permute-start | bytes 1572872 | tf_op jit(solution)/shard_map/ppermute | solution.py:220
  154.6 6.3 %copy-start.9 = (s32[1,1,24,1]{2,3,1,0:T(1,128)S(1)}, s32[1,1,24,1]{2,3,1,0:T(1,128)}, u32[]{:S(2)}) copy-start(s32[1,1,24,1]{2,3,1,0:T(1,128)} %param.23) | copy-start | bytes 292
  154.6 6.5 %copy-start.8 = (s32[1,1,24,2]{2,3,1,0:T(2,128)S(1)}, s32[1,1,24,2]{2,3,1,0:T(2,128)}, u32[]{:S(2)}) copy-start(s32[1,1,24,2]{2,3,1,0:T(2,128)} %param.22) | copy-start | bytes 580
  154.8 12.4 %collective-permute-start.2 = (f32[2,128,768]{2,1,0:T(8,128)S(1)}, f32[2,128,768]{2,1,0:T(8,128)S(1)}, u32[]{:S(2)}, u32[]{:S(2)}) collective-permute-start(f32[2,128,768]{2,1,0:T(8,128)S(1)} %get-tuple-element.57), channel_id=1, source_target_pairs={{0,1},{1,2},{2,3},{4,5},{5,6},{6,7},{8,9},{9,10},{10,11},{12,13},{... | collective-permute-start | bytes 2359304 | tf_op jit(solution)/shard_map/ppermute | solution.py:220
  158.3 13.3 %collective-permute-start.3 = (f32[2,128,768]{2,1,0:T(8,128)S(1)}, f32[2,128,768]{2,1,0:T(8,128)S(1)}, u32[]{:S(2)}, u32[]{:S(2)}) collective-permute-start(f32[2,128,768]{2,1,0:T(8,128)S(1)} %get-tuple-element.58), channel_id=1, source_target_pairs={{1,0},{2,1},{3,2},{5,4},{6,5},{7,6},{9,8},{10,9},{11,10},{13,12},{... | collective-permute-start | bytes 2359304 | tf_op jit(solution)/shard_map/ppermute | solution.py:220
  161.1 10.8 %copy-start = (f32[2,256,256]{2,1,0:T(8,128)S(1)}, f32[2,256,256]{2,1,0:T(8,128)}, u32[]{:S(2)}) copy-start(f32[2,256,256]{2,1,0:T(8,128)} %probe_ref.3) | copy-start | bytes 1572868
  161.2 10.8 %copy-start.1 = (bf16[2,256,768]{2,1,0:T(8,128)(2,1)S(1)}, bf16[2,256,768]{2,1,0:T(8,128)(2,1)}, u32[]{:S(2)}) copy-start(bf16[2,256,768]{2,1,0:T(8,128)(2,1)} %constant.127.clone.left_ref) | copy-start | bytes 2359300
  161.2 10.8 %copy-start.4 = (bf16[2,768,256]{2,1,0:T(8,128)(2,1)S(1)}, bf16[2,768,256]{2,1,0:T(8,128)(2,1)}, u32[]{:S(2)}) copy-start(bf16[2,768,256]{2,1,0:T(8,128)(2,1)} %constant.125.clone.right_ref) | copy-start | bytes 2359300
  172.0 26.4 %copy-start.2 = (bf16[2,256,768]{2,1,0:T(8,128)(2,1)S(1)}, bf16[2,256,768]{2,1,0:T(8,128)(2,1)}, u32[]{:S(2)}) copy-start(bf16[2,256,768]{2,1,0:T(8,128)(2,1)} %constant.128.clone.left_ref) | copy-start | bytes 2359300
  172.0 26.4 %copy-start.3 = (bf16[2,768,256]{2,1,0:T(8,128)(2,1)S(1)}, bf16[2,768,256]{2,1,0:T(8,128)(2,1)}, u32[]{:S(2)}) copy-start(bf16[2,768,256]{2,1,0:T(8,128)(2,1)} %constant.126.clone.right_ref) | copy-start | bytes 2359300
  172.0 26.4 %copy-start.5 = (bf16[512,256]{1,0:T(8,128)(2,1)S(1)}, bf16[512,256]{1,0:T(8,128)(2,1)}, u32[]{:S(2)}) copy-start(bf16[512,256]{1,0:T(8,128)(2,1)} %constant.129.clone.perm_ref) | copy-start | bytes 786436
  233.3 13.7 %collective-permute-start.4 = (f32[2,768,128]{2,1,0:T(8,128)S(1)}, f32[2,768,128]{2,1,0:T(8,128)S(1)}, u32[]{:S(2)}, u32[]{:S(2)}) collective-permute-start(f32[2,768,128]{2,1,0:T(8,128)S(1)} %get-tuple-element.54), channel_id=1, source_target_pairs={{0,4},{4,8},{8,12},{12,16},{16,20},{20,24},{24,28},{1,5},{5,9},{9,... | collective-permute-start | bytes 2359304 | tf_op jit(solution)/shard_map/ppermute | solution.py:220
  235.3 20.1 %collective-permute-start.5 = (f32[2,768,128]{2,1,0:T(8,128)S(1)}, f32[2,768,128]{2,1,0:T(8,128)S(1)}, u32[]{:S(2)}, u32[]{:S(2)}) collective-permute-start(f32[2,768,128]{2,1,0:T(8,128)S(1)} %get-tuple-element.53), channel_id=1, source_target_pairs={{4,0},{8,4},{12,8},{16,12},{20,16},{24,20},{28,24},{5,1},{9,5},{13... | collective-permute-start | bytes 2359304 | tf_op jit(solution)/shard_map/ppermute | solution.py:220
  255.6 9.0 %collective-permute-start.6 = (f32[2,128,512]{2,1,0:T(8,128)S(1)}, f32[2,128,512]{2,1,0:T(8,128)S(1)}, u32[]{:S(2)}, u32[]{:S(2)}) collective-permute-start(f32[2,128,512]{2,1,0:T(8,128)S(1)} %get-tuple-element.56), channel_id=1, source_target_pairs={{0,1},{1,2},{2,3},{4,5},{5,6},{6,7},{8,9},{9,10},{10,11},{12,13},{... | collective-permute-start | bytes 1572872 | tf_op jit(solution)/shard_map/ppermute | solution.py:220
  258.6 10.8 %copy-start.7 = (f32[2,512,512]{2,1,0:T(8,128)S(1)}, f32[2,512,512]{2,1,0:T(8,128)}, u32[]{:S(2)}) copy-start(f32[2,512,512]{2,1,0:T(8,128)} %param.19) | copy-start | bytes 6291460
  258.6 10.6 %collective-permute-start.7 = (f32[2,128,512]{2,1,0:T(8,128)S(1)}, f32[2,128,512]{2,1,0:T(8,128)S(1)}, u32[]{:S(2)}, u32[]{:S(2)}) collective-permute-start(f32[2,128,512]{2,1,0:T(8,128)S(1)} %get-tuple-element.55), channel_id=1, source_target_pairs={{1,0},{2,1},{3,2},{5,4},{6,5},{7,6},{9,8},{10,9},{11,10},{13,12},{... | collective-permute-start | bytes 1572872 | tf_op jit(solution)/shard_map/ppermute | solution.py:220

commit v2 on v1

--- a/solution.py
+++ b/solution.py
@@ -120,21 +120,29 @@
         )
 
 
-def backward_kernel(
-    blocks, info_ref, far_ref, frame_ref, probe_ref, right_ref, left_ref, perm_ref, grad_ref, sorted_ref
-):
+def backward_kernel(blocks, chunks, begun, info_ref, far_ref, *refs):
+    frame_refs, refs = refs[:chunks], refs[chunks:]
+    probe_ref, right_ref, left_ref, perm_ref = refs[:4]
+    grad_ref, sorted_ref, frame_ref = refs[-3:]
+    slots = pl.num_programs(0) // chunks
     size = probe_ref.shape[1]
     half = size // 2
     index = pl.program_id(0)
 
     @pl.when(index == 0)
     def _():
-        grad_ref[...] = jnp.zeros_like(grad_ref)
+        grad_ref[...] = refs[4][...] if begun else jnp.zeros_like(grad_ref)
+
+    for chunk in range(chunks):
+
+        @pl.when(index // slots == chunk)
+        def _():
+            frame_ref[...] = frame_refs[chunk][0]
 
     @pl.when(info_ref[2, index] > 0)
     def _():
         ys, xs, a_y, a_x = place(info_ref, index, size, blocks)
-        hi, lo = halves(frame_ref[0])
+        hi, lo = halves(frame_ref[...])
         frame = jnp.dot(jnp.concatenate([hi, lo], axis=1), perm_ref[...], preferred_element_type=f32)
         sorted_ref[0] = frame[:, :half]
         sorted_ref[1] = frame[:, half:]
@@ -189,28 +197,34 @@
     )(info, field, probe, right, left)
 
 
-def run_backward(info, far, frames, probe, right, left, perm, extent):
-    count, size = info.shape[1], probe.shape[1]
+def run_backward(info, first, far, frames, probe, right, left, perm, extent, grad):
+    slots, size = frames[0].shape[:2]
+    count = slots * len(frames)
+    tables = [probe, right, left, perm] + ([] if grad is None else [grad])
+
+    def frame_spec(chunk):
+        return pl.BlockSpec(
+            (1, size, size), lambda i, info: (jnp.clip(i - chunk * slots, 0, slots - 1), 0, 0)
+        )
+
     return pl.pallas_call(
-        functools.partial(backward_kernel, extent // size),
+        functools.partial(backward_kernel, extent // size, len(frames), grad is not None),
         out_shape=jax.ShapeDtypeStruct((2, extent, extent), f32),
         grid_spec=pltpu.PrefetchScalarGridSpec(
             num_scalar_prefetch=1,
             grid=(count,),
-            in_specs=[
-                pl.BlockSpec((1, 2, size, size), lambda i, info: (i, 0, 0, 0)),
-                pl.BlockSpec((1, size, size), lambda i, info: (info[3, i], 0, 0)),
-                whole(probe.shape), whole(right.shape), whole(left.shape), whole(perm.shape),
-            ],
+            in_specs=[pl.BlockSpec((1, 2, size, size), lambda i, info: (first + i, 0, 0, 0))]
+            + [frame_spec(chunk) for chunk in range(len(frames))]
+            + [whole(table.shape) for table in tables],
             out_specs=whole((2, extent, extent)),
-            scratch_shapes=[pltpu.VMEM((2, size, size // 2), f32)],
+            scratch_shapes=[pltpu.VMEM((2, size, size // 2), f32), pltpu.VMEM((size, size), f32)],
         ),
         compiler_params=pltpu.CompilerParams(vmem_limit_bytes=40 << 20),
         cost_estimate=pl.CostEstimate(
             flops=count * 24 * size**3, bytes_accessed=4 * count * 3 * size**2, transcendentals=0
         ),
         name="backward",
-    )(info, far, frames, probe, right, left, perm)
+    )(info[:, first : first + count], far, *frames, *tables)
 
 
 def from_sides(low_part, high_part, axis):
@@ -226,10 +240,27 @@
     extent = tile + 2 * half
     kept = frames[0, 0]
     sources, slots = kept.shape[:2]
-    fetched = lax.all_to_all(kept, "gx", split_axis=0, concat_axis=0, tiled=True)
-    fetched = fetched.reshape(sources * slots, size, size)
+    me = lax.axis_index("gx")
+    paired = sources & (sources - 1) == 0
+    ids = list(range(sources))
+
+    def target_of(d, i):
+        return i ^ d if paired else (i + d) % sources
+
+    def source_of(d, i):
+        return i ^ d if paired else (i - d + sources) % sources
+
+    far_steps, near_steps = ids[sources // 2 :], ids[1 : sources // 2]
+    order = []
+    for number, d in enumerate(far_steps):
+        order += [d] + near_steps[number : number + 1]
+    groups = [[0] + order[:2]] + [order[i : i + 2] for i in range(2, len(order), 2)]
+    groups = [group for group in groups if group]
+    order = [d for group in groups for d in group]
 
     before, after = from_sides(object_field[:, :, :half], object_field[:, :, tile - half :], "gx")
+    early = me
+    late, before, after = lax.optimization_barrier((me, before, after))
     field = jnp.concatenate([before, object_field, after], axis=2)
     before, after = from_sides(field[:, :half], field[:, tile - half :], "gy")
     field = jnp.concatenate([before, field, after], axis=1)
@@ -241,22 +272,50 @@
     helper_cols = helpers[0, 0, :, 0]
     same = helper_cols[:, None] == helper_cols[None, :]
     ranks = jnp.sum(jnp.logical_and(same, task_ids[None, :] < task_ids[:, None]), axis=1)
+    slot_of = helper_cols * slots + ranks
+    kinds = jnp.concatenate(
+        [source_of(d, me) * slots + jnp.arange(slots, dtype=jnp.int32) for d in order]
+    )
+    hit = jnp.logical_and(slot_of[None, :] == kinds[:, None], valid[None, :]).astype(jnp.int32)
     info = jnp.stack(
-        [offsets[:, 0] + half, offsets[:, 1] + half, valid.astype(jnp.int32), helper_cols * slots + ranks]
+        [
+            jnp.sum(hit * (offsets[None, :, 0] + half), axis=1),
+            jnp.sum(hit * (offsets[None, :, 1] + half), axis=1),
+            jnp.sum(hit, axis=1),
+        ]
     ).astype(jnp.int32)
 
     right, right_t, left, left_t, perm = (jnp.asarray(t) for t in dft_tables(size))
     far = run_forward(info, field, probe, right, left)
-    summed = run_backward(info, far, fetched, probe, right_t, left_t, perm, extent)
-
-    before, after = from_sides(summed[:, :, :half], summed[:, :, tile + half :], "gx")
-    middle = summed[:, :, half : half + tile]
-    middle = middle.at[:, :, :half].add(before)
-    middle = middle.at[:, :, tile - half :].add(after)
-    before, after = from_sides(middle[:, :half], middle[:, tile + half :], "gy")
-    gradient = middle[:, half : half + tile]
-    gradient = gradient.at[:, :half].add(before)
-    gradient = gradient.at[:, tile - half :].add(after)
+    arrived = {}
+    for number, d in enumerate(order):
+        at = early if number < 3 else late
+        if number >= 5:
+            past = order[number - 4]
+            at, arrived[past] = lax.optimization_barrier((at, arrived[past]))
+        chunk = lax.dynamic_index_in_dim(kept, target_of(d, at), axis=0, keepdims=False)
+        arrived[d] = chunk if d == 0 else lax.ppermute(chunk, "gx", [(i, target_of(d, i)) for i in ids])
+
+    summed, first = None, 0
+    for group in groups:
+        summed = run_backward(
+            info, first, far, [arrived[d] for d in group], probe, right_t, left_t, perm, extent, summed
+        )
+        first += len(group) * slots
+
+    west, east = from_sides(summed[:, :, :half], summed[:, :, tile + half :], "gx")
+    inner = summed[:, :, half : half + tile]
+    north, south = from_sides(inner[:, :half], inner[:, tile + half :], "gy")
+    corners = jnp.concatenate([west, east], axis=2)
+    corner_north, corner_south = from_sides(corners[:, :half], corners[:, tile + half :], "gy")
+    gradient = inner[:, half : half + tile]
+    gradient = gradient.at[:, :half].add(north)
+    gradient = gradient.at[:, tile - half :].add(south)
+    side = corners[:, half : half + tile]
+    side = side.at[:, :half].add(corner_north)
+    side = side.at[:, tile - half :].add(corner_south)
+    gradient = gradient.at[:, :, :half].add(side[:, :, :half])
+    gradient = gradient.at[:, :, tile - half :].add(side[:, :, half:])
     return object_field - step_size * (gradient + ridge * object_field)
 
 

time: 272 us -> 258 us (0.949)
  waiting for transfers between devices: 176 us -> 131 us
  starting transfers between devices: 28.5 us -> 43.2 us
  local copies, waits for them, and re-layouts: 1.23 us -> 12.5 us
  Pallas kernels: 61.2 us -> 64.1 us
    ppermute x4 -> x5, waiting for transfers between devices: 159 us -> 31.3 us  [from_sides(): lax.ppermute(high_part, axis, forward)]
    ppermute x0 -> x7, waiting for transfers between devices: none -> 76.5 us  [per_device(): lax.ppermute(chunk, 'gx', [(i, target_of(d, i)) for i in ids])]
    ppermute x0 -> x7, starting transfers between devices: none -> 10.6 us  [per_device(): lax.ppermute(chunk, 'gx', [(i, target_of(d, i)) for i in ids])]
    ppermute x4 -> x5, starting transfers between devices: 11.4 us -> 19.4 us  [from_sides(): lax.ppermute(high_part, axis, forward)]
    ppermute x4 -> x5, waiting for transfers between devices: 17 us -> 23.4 us  [from_sides(): lax.ppermute(low_part, axis, backward)]
    squeeze x0 -> x2, local copies, waits for them, and re-layouts: none -> 5.83 us  [per_device(): lax.dynamic_index_in_dim(kept, target_of(d, at), axis=0, keepdims=False)]
    all_to_all x1 -> x0, starting transfers between devices: 5.74 us -> none  [per_device(): lax.all_to_all(kept, 'gx', split_axis=0, concat_axis=0, tiled=True)]
    pallas_call x1 -> x4, Pallas kernels: 34.8 us -> 37.9 us  [run_backward(): pl.pallas_call(functools.partial(backward_kernel, extent // size, len(fra...]
  transfers between devices with their start and end apart: 9 -> 17, of which waited for: 7 -> 9; matrix products, arithmetic and copies ran while one was open for 1% -> 3% of each run, Pallas kernels for 10% -> 23%
where the time goes in v2:
time: 258 us; the launch traced here: 256 us
  waiting for transfers between devices  131 us (51%)
  Pallas kernels  64.1 us (25%)
  starting transfers between devices  43.2 us (17%)
  local copies, waits for them, and re-layouts  12.5 us (5%)
  other arithmetic  4.34 us (2%)
    ppermute x7, waiting for transfers between devices, per_device(): lax.ppermute(chunk, 'gx', [(i, target_of(d, i)) for i in ids])  76.5 us
    pallas_call x4, Pallas kernels, run_backward(): pl.pallas_call(functools.partial(backward_kernel, extent // size, len(fra...  37.9 us
    ppermute x5, waiting for transfers between devices, from_sides(): lax.ppermute(high_part, axis, forward)  31.3 us
    pallas_call x1, Pallas kernels, run_forward(): pl.pallas_call(functools.partial(forward_kernel, field.shape[1] // size),...  26.1 us
    ppermute x5, waiting for transfers between devices, from_sides(): lax.ppermute(low_part, axis, backward)  23.4 us
    ppermute x5, starting transfers between devices, from_sides(): lax.ppermute(high_part, axis, forward)  19.4 us
    ppermute x5, starting transfers between devices, from_sides(): lax.ppermute(low_part, axis, backward)  13.2 us
    ppermute x7, starting transfers between devices, per_device(): lax.ppermute(chunk, 'gx', [(i, target_of(d, i)) for i in ids])  10.6 us
  transfers between devices with their start and end apart: 17, of which 9 were waited for; matrix products, arithmetic and copies ran while one was open for 3% of the time, Pallas kernels for 23%

profile of v2, /device:TPU:17, one launch (start us, length us, event | category | flops | bytes accessed | tf_op | source)
XLA Modules:
  0.0 256.4 jit_solution(18443557049402668192)
XLA Ops:
  0.0 1.3 fusion.10
  1.3 3.0 %collective-permute-start.1 = (f32[2,512,128]{2,1,0:T(8,128)S(1)}, f32[2,512,128]{2,1,0:T(8,128)S(1)}, u32[]{:S(2)}, u32[]{:S(2)}) collective-permute-start(f32[2,512,128]{2,1,0:T(8,128)S(1)} %get-tuple-element.112), channel_id=1, source_target_pairs={{4,0},{8,4},{12,8},{16,12},{20,16},{24,20},{28,24},{5,1},{9,5},{13... | collective-permute-start | bytes 1572872 | tf_op jit(solution)/shard_map/ppermute | solution.py:234
  4.4 2.2 collective-permute-start
  6.7 0.2 convert_reduce_fusion.1
  6.9 20.3 %collective-permute-done.1 = f32[2,512,128]{2,1,0:T(8,128)S(1)} collective-permute-done((f32[2,512,128]{2,1,0:T(8,128)S(1)}, f32[2,512,128]{2,1,0:T(8,128)S(1)}, u32[]{:S(2)}, u32[]{:S(2)}) %collective-permute-start.1) | collective-permute-done | bytes 524320 | tf_op jit(solution)/shard_map/ppermute | solution.py:234
  27.2 1.0 collective-permute-done
  28.2 3.3 %dynamic-slice_bitcast_fusion.3 = (f32[3,256,256]{2,1,0:T(8,128)}, f32[3,256,256]{2,1,0:T(8,128)}, f32[3,256,256]{2,1,0:T(8,128)}) fusion(f32[1,1,8,3,256,256]{5,4,3,2,1,0:T(8,128)} %param.25, s32[]{:T(128)S(6)} %select_n.29, s32[]{:T(128)S(6)} %select_n.27, s32[]{:T(128)S(6)} %select_n.25), kind=kLoop, calls=%fused_computation.5 | loop fusion | bytes 4718604 | tf_op jit(solution)/shard_map/jit(dynamic_index_in_dim)/squeeze | solution.py:296
  31.5 2.2 collective-permute-start.8
  33.7 0.1 collective-permute-start.6
  33.7 2.0 collective-permute-start.4
  35.8 0.2 constant_dynamic-update-slice_fusion.1
  36.1 1.6 copy-done.8
  37.7 1.3 fusion.9
  39.0 4.0 %collective-permute-start.2 = (f32[2,128,768]{2,1,0:T(8,128)}, f32[2,128,768]{2,1,0:T(8,128)S(1)}, u32[]{:S(2)}, u32[]{:S(2)}) collective-permute-start(f32[2,128,768]{2,1,0:T(8,128)} %get-tuple-element.110), channel_id=1, source_target_pairs={{0,1},{1,2},{2,3},{4,5},{5,6},{6,7},{8,9},{9,10},{10,11},{12,13},{... | collective-permute-start | bytes 2359304 | tf_op jit(solution)/shard_map/ppermute | solution.py:234
  43.0 1.9 collective-permute-start.3
  45.6 0.1 concatenate.24
  45.7 0.2 select_reduce_fusion.1
  45.9 0.1 slice.212.info_ref
  46.0 0.1 fusion.12
  46.1 5.3 %collective-permute-done.8.refs_2_ = f32[3,256,256]{2,1,0:T(8,128)S(1)} collective-permute-done((f32[3,256,256]{2,1,0:T(8,128)}, f32[3,256,256]{2,1,0:T(8,128)S(1)}, u32[]{:S(2)}, u32[]{:S(2)}) %collective-permute-start.8) | collective-permute-done | bytes 786464 | tf_op jit(solution)/shard_map/ppermute | solution.py:297
  51.4 32.6 %collective-permute-done.6.refs_1_ = f32[3,256,256]{2,1,0:T(8,128)S(1)} collective-permute-done((f32[3,256,256]{2,1,0:T(8,128)}, f32[3,256,256]{2,1,0:T(8,128)S(1)}, u32[]{:S(2)}, u32[]{:S(2)}) %collective-permute-start.6) | collective-permute-done | bytes 786464 | tf_op jit(solution)/shard_map/ppermute | solution.py:297
  84.0 16.9 %collective-permute-done.4.refs_0_ = f32[3,256,256]{2,1,0:T(8,128)S(1)} collective-permute-done((f32[3,256,256]{2,1,0:T(8,128)}, f32[3,256,256]{2,1,0:T(8,128)S(1)}, u32[]{:S(2)}, u32[]{:S(2)}) %collective-permute-start.4) | collective-permute-done | bytes 786464 | tf_op jit(solution)/shard_map/ppermute | solution.py:297
  100.8 2.6 %dynamic-slice_bitcast_fusion = (f32[3,256,256]{2,1,0:T(8,128)S(1)}, f32[3,256,256]{2,1,0:T(8,128)S(1)}, f32[3,256,256]{2,1,0:T(8,128)S(1)}, f32[3,256,256]{2,1,0:T(8,128)S(1)}, f32[3,256,256]{2,1,0:T(8,128)S(1)}) fusion(f32[1,1,8,3,256,256]{5,4,3,2,1,0:T(8,128)} %param.25, s32[]{:T(128)S(6)} %select_n.32, s32[]{:T(128)S(6)} %select_n.30, s32[]{:T(128)S(6)} %select_n.28, ...), kind=kLoop, calls=%fused_computation.2 | loop fusion | bytes 7864340 | tf_op jit(solution)/shard_map/jit(dynamic_index_in_dim)/squeeze | solution.py:296
  103.4 2.9 %collective-permute-start.9 = (f32[3,256,256]{2,1,0:T(8,128)S(1)}, f32[3,256,256]{2,1,0:T(8,128)S(1)}, u32[]{:S(2)}, u32[]{:S(2)}) collective-permute-start(f32[3,256,256]{2,1,0:T(8,128)S(1)} %get-tuple-element.99), channel_id=1, source_target_pairs={{0,12},{4,8},{8,4},{12,0},{16,28},{20,24},{24,20},{28,16},{1,13},{... | collective-permute-start | bytes 2359304 | tf_op jit(solution)/shard_map/ppermute | solution.py:297
  106.3 1.3 collective-permute-start.7
  107.7 0.0 collective-permute-start.5
  107.7 0.0 collective-permute-done.2
  107.7 0.0 copy-start.4
  107.7 0.0 copy-start.5
  107.7 2.0 collective-permute-start.10
  109.7 0.0 collective-permute-done.3
  109.7 1.4 pad_maximum_fusion.field_ref
  111.2 0.0 copy-start
  111.2 0.0 copy-start.1
  111.2 0.0 copy-start.3
  111.3 26.1 %forward.1.far_ref = f32[24,2,256,256]{3,2,1,0:T(8,128)} custom-call(s32[3,24]{1,0:T(4,128)S(1)} %pad_add_fusion.info_ref, f32[2,768,768]{2,1,0:T(8,128)S(1)} %pad_maximum_fusion.field_ref, f32[2,256,256]{2,1,0:T(8,128)S(1)} %copy-done.2, bf16[2,768,256]{2,1,0:T(8,128)(2,1)S(1)} %copy-done.5, bf16[2,256,768]{2,1,0:T(8,128)(2,1)S(1)} %copy-done.4), custom_call_target="tpu_custom_call" | custom-call | flops 9663676416 | bytes 17301504 | tf_op jit(solution)/shard_map/forward/pallas_call | solution.py:183
  137.4 13.0 %backward.4.refs_6_ = f32[2,768,768]{2,1,0:T(8,128)S(1)} custom-call(s32[3,9]{1,0:T(4,128)S(1)} %bitcast.29, f32[24,2,256,256]{3,2,1,0:T(8,128)} %forward.1.far_ref, f32[3,256,256]{2,1,0:T(8,128)S(1)} %get-tuple-element.98.refs_0_, f32[3,256,256]{2,1,0:T(8,128)S(1)} %collective-permute-done.6.refs_1_, f32[3,256,256]{2,1,0:T(8,128)S(1)} %collective-permute-done.8.refs_2_, ...), custom_call_target="tpu_custom_call" | custom-call | flops 3623878656 | bytes 7077888 | tf_op jit(solution)/shard_map/backward/pallas_call | solution.py:210
  150.4 21.8 %collective-permute-done.10.refs_1_ = f32[3,256,256]{2,1,0:T(8,128)S(1)} collective-permute-done((f32[3,256,256]{2,1,0:T(8,128)S(1)}, f32[3,256,256]{2,1,0:T(8,128)S(1)}, u32[]{:S(2)}, u32[]{:S(2)}) %collective-permute-start.10) | collective-permute-done | bytes 786464 | tf_op jit(solution)/shard_map/ppermute | solution.py:297
  172.2 9.4 %backward.5.refs_6_ = f32[2,768,768]{2,1,0:T(8,128)S(1)} custom-call(s32[3,6]{1,0:T(4,128)S(1)} %get-tuple-element.116.info_ref, f32[24,2,256,256]{3,2,1,0:T(8,128)} %forward.1.far_ref, f32[3,256,256]{2,1,0:T(8,128)S(1)} %collective-permute-done.4.refs_0_, f32[3,256,256]{2,1,0:T(8,128)S(1)} %collective-permute-done.10.refs_1_, f32[2,256,256]{2,1,0:T(8,128)S(1)} %copy-done.2, ...), custom_call_target="tpu_custom_call" | custom-call | flops 2415919104 | bytes 4718592 | tf_op jit(solution)/shard_map/backward/pallas_call | solution.py:210
  181.6 0.0 collective-permute-done.9.refs_1_
  181.6 10.5 %backward.6.refs_5_ = f32[2,768,768]{2,1,0:T(8,128)S(1)} custom-call(s32[3,6]{1,0:T(4,128)S(1)} %get-tuple-element.117.info_ref, f32[24,2,256,256]{3,2,1,0:T(8,128)} %forward.1.far_ref, f32[3,256,256]{2,1,0:T(8,128)} %collective-permute-done.7.refs_0_, f32[3,256,256]{2,1,0:T(8,128)S(1)} %collective-permute-done.9.refs_1_, f32[2,256,256]{2,1,0:T(8,128)S(1)} %copy-done.2, ...), custom_call_target="tpu_custom_call" | custom-call | flops 2415919104 | bytes 4718592 | tf_op jit(solution)/shard_map/backward/pallas_call | solution.py:210
  192.2 5.0 %backward.7 = f32[2,768,768]{2,1,0:T(8,128)S(1)} custom-call(s32[3,3]{1,0:T(4,128)S(1)} %slice.212.info_ref, f32[24,2,256,256]{3,2,1,0:T(8,128)} %forward.1.far_ref, f32[3,256,256]{2,1,0:T(8,128)S(1)} %collective-permute-done.5.refs_0_, f32[2,256,256]{2,1,0:T(8,128)S(1)} %copy-done.2, bf16[2,768,256]{2,1,0:T(8,128)(2,1)S(1)} %copy-done.1, ...), custom_call_target="tpu_custom_call" | custom-call | flops 1207959552 | bytes 2359296 | tf_op jit(solution)/shard_map/backward/pallas_call | solution.py:210
  197.2 0.1 fusion.8
  197.3 7.4 %collective-permute-start.11 = (f32[2,128,512]{2,1,0:T(8,128)S(1)}, f32[2,128,512]{2,1,0:T(8,128)S(1)}, u32[]{:S(2)}, u32[]{:S(2)}) collective-permute-start(f32[2,128,512]{2,1,0:T(8,128)S(1)} %get-tuple-element.109), channel_id=1, source_target_pairs={{0,1},{1,2},{2,3},{4,5},{5,6},{6,7},{8,9},{9,10},{10,11},{12,13},{... | collective-permute-start | bytes 1572872 | tf_op jit(solution)/shard_map/ppermute | solution.py:234
  204.7 0.1 fusion.7
  204.8 2.5 collective-permute-start.13
  207.3 3.7 %collective-permute-start.14 = (f32[2,768,128]{2,1,0:T(8,128)S(1)}, f32[2,768,128]{2,1,0:T(8,128)S(1)}, u32[]{:S(2)}, u32[]{:S(2)}) collective-permute-start(f32[2,768,128]{2,1,0:T(8,128)S(1)} %get-tuple-element.106), channel_id=1, source_target_pairs={{4,0},{8,4},{12,8},{16,12},{20,16},{24,20},{28,24},{5,1},{9,5},{13... | collective-permute-start | bytes 2359304 | tf_op jit(solution)/shard_map/ppermute | solution.py:234
  211.0 0.3 slice.238
  211.2 2.2 collective-permute-start.12
  213.5 0.1 fusion.3
  213.6 27.3 %collective-permute-done.13 = f32[2,768,128]{2,1,0:T(8,128)S(1)} collective-permute-done((f32[2,768,128]{2,1,0:T(8,128)S(1)}, f32[2,768,128]{2,1,0:T(8,128)S(1)}, u32[]{:S(2)}, u32[]{:S(2)}) %collective-permute-start.13) | collective-permute-done | bytes 786464 | tf_op jit(solution)/shard_map/ppermute | solution.py:234
  240.8 0.1 constant_dynamic-update-slice_fusion.4
  240.9 3.1 %collective-permute-done.14 = f32[2,768,128]{2,1,0:T(8,128)S(1)} collective-permute-done((f32[2,768,128]{2,1,0:T(8,128)S(1)}, f32[2,768,128]{2,1,0:T(8,128)S(1)}, u32[]{:S(2)}, u32[]{:S(2)}) %collective-permute-start.14) | collective-permute-done | bytes 786464 | tf_op jit(solution)/shard_map/ppermute | solution.py:234
  244.0 0.1 constant_dynamic-update-slice_fusion.3
  244.1 2.3 collective-permute-start.16
  246.4 3.3 %collective-permute-start.15 = (f32[2,128,256]{2,1,0:T(8,128)S(1)}, f32[2,128,256]{2,1,0:T(8,128)S(1)}, u32[]{:S(2)}, u32[]{:S(2)}) collective-permute-start(f32[2,128,256]{2,1,0:T(8,128)S(1)} %get-tuple-element.115), channel_id=1, source_target_pairs={{0,1},{1,2},{2,3},{4,5},{5,6},{6,7},{8,9},{9,10},{10,11},{12,13},{... | collective-permute-start | bytes 786440 | tf_op jit(solution)/shard_map/ppermute | solution.py:234
  249.7 0.1 fusion.2
  249.8 0.1 slice.246
  249.9 3.1 %collective-permute-done.15 = f32[2,128,256]{2,1,0:T(8,128)S(1)} collective-permute-done((f32[2,128,256]{2,1,0:T(8,128)S(1)}, f32[2,128,256]{2,1,0:T(8,128)S(1)}, u32[]{:S(2)}, u32[]{:S(2)}) %collective-permute-start.15) | collective-permute-done | bytes 262176 | tf_op jit(solution)/shard_map/ppermute | solution.py:234
  253.0 0.1 fusion.4
  253.1 0.1 fusion.1
  253.2 0.1 fusion
  253.4 1.2 copy-done.7
  254.6 1.8 multiply_subtract_fusion
  (35 shorter events, 0.3 us)
Async XLA Ops:
  0.0 6.7 %copy-start.11 = (s32[1,1,24,1]{2,3,1,0:T(1,128)S(1)}, s32[1,1,24,1]{2,3,1,0:T(1,128)}, u32[]{:S(2)}) copy-start(s32[1,1,24,1]{2,3,1,0:T(1,128)} %param.27) | copy-start | bytes 292
  0.0 6.9 %copy-start.10 = (s32[1,1,24,2]{2,3,1,0:T(2,128)S(1)}, s32[1,1,24,2]{2,3,1,0:T(2,128)}, u32[]{:S(2)}) copy-start(s32[1,1,24,2]{2,3,1,0:T(2,128)} %param.26) | copy-start | bytes 580
  1.3 25.9 %collective-permute-start.1 = (f32[2,512,128]{2,1,0:T(8,128)S(1)}, f32[2,512,128]{2,1,0:T(8,128)S(1)}, u32[]{:S(2)}, u32[]{:S(2)}) collective-permute-start(f32[2,512,128]{2,1,0:T(8,128)S(1)} %get-tuple-element.112), channel_id=1, source_target_pairs={{4,0},{8,4},{12,8},{16,12},{20,16},{24,20},{28,24},{5,1},{9,5},{13... | collective-permute-start | bytes 1572872 | tf_op jit(solution)/shard_map/ppermute | solution.py:234
  4.4 23.9 %collective-permute-start = (f32[2,512,128]{2,1,0:T(8,128)S(1)}, f32[2,512,128]{2,1,0:T(8,128)S(1)}, u32[]{:S(2)}, u32[]{:S(2)}) collective-permute-start(f32[2,512,128]{2,1,0:T(8,128)S(1)} %get-tuple-element.113), channel_id=1, source_target_pairs={{0,4},{4,8},{8,12},{12,16},{16,20},{20,24},{24,28},{1,5},{5,9},{9,... | collective-permute-start | bytes 1572872 | tf_op jit(solution)/shard_map/ppermute | solution.py:234
  28.2 7.6 %copy-start.6 = (f32[2,512,512]{2,1,0:T(8,128)S(1)}, f32[2,512,512]{2,1,0:T(8,128)}, u32[]{:S(2)}) copy-start(f32[2,512,512]{2,1,0:T(8,128)} %param.23) | copy-start | bytes 6291460
  31.5 19.9 %collective-permute-start.8 = (f32[3,256,256]{2,1,0:T(8,128)}, f32[3,256,256]{2,1,0:T(8,128)S(1)}, u32[]{:S(2)}, u32[]{:S(2)}) collective-permute-start(f32[3,256,256]{2,1,0:T(8,128)} %get-tuple-element.103), channel_id=1, source_target_pairs={{0,4},{4,0},{8,12},{12,8},{16,20},{20,16},{24,28},{28,24},{1,5},{5... | collective-permute-start | bytes 2359304 | tf_op jit(solution)/shard_map/ppermute | solution.py:297
  33.7 50.3 %collective-permute-start.6 = (f32[3,256,256]{2,1,0:T(8,128)}, f32[3,256,256]{2,1,0:T(8,128)S(1)}, u32[]{:S(2)}, u32[]{:S(2)}) collective-permute-start(f32[3,256,256]{2,1,0:T(8,128)} %get-tuple-element.104), channel_id=1, source_target_pairs={{0,16},{4,20},{8,24},{12,28},{16,0},{20,4},{24,8},{28,12},{1,17},{... | collective-permute-start | bytes 2359304 | tf_op jit(solution)/shard_map/ppermute | solution.py:297
  33.7 67.1 %collective-permute-start.4 = (f32[3,256,256]{2,1,0:T(8,128)}, f32[3,256,256]{2,1,0:T(8,128)S(1)}, u32[]{:S(2)}, u32[]{:S(2)}) collective-permute-start(f32[3,256,256]{2,1,0:T(8,128)} %get-tuple-element.105), channel_id=1, source_target_pairs={{0,20},{4,16},{8,28},{12,24},{16,4},{20,0},{24,12},{28,8},{1,21},{... | collective-permute-start | bytes 2359304 | tf_op jit(solution)/shard_map/ppermute | solution.py:297
  36.1 1.6 copy-start.8
  39.0 68.7 %collective-permute-start.2 = (f32[2,128,768]{2,1,0:T(8,128)}, f32[2,128,768]{2,1,0:T(8,128)S(1)}, u32[]{:S(2)}, u32[]{:S(2)}) collective-permute-start(f32[2,128,768]{2,1,0:T(8,128)} %get-tuple-element.110), channel_id=1, source_target_pairs={{0,1},{1,2},{2,3},{4,5},{5,6},{6,7},{8,9},{9,10},{10,11},{12,13},{... | collective-permute-start | bytes 2359304 | tf_op jit(solution)/shard_map/ppermute | solution.py:234
  43.0 66.7 %collective-permute-start.3 = (f32[2,128,768]{2,1,0:T(8,128)}, f32[2,128,768]{2,1,0:T(8,128)}, u32[]{:S(2)}, u32[]{:S(2)}) collective-permute-start(f32[2,128,768]{2,1,0:T(8,128)} %get-tuple-element.111), channel_id=1, source_target_pairs={{1,0},{2,1},{3,2},{5,4},{6,5},{7,6},{9,8},{10,9},{11,10},{13,12},{... | collective-permute-start | bytes 2359304 | tf_op jit(solution)/shard_map/ppermute | solution.py:234
  100.8 8.9 %copy-start.9 = (f32[2,512,768]{2,1,0:T(8,128)S(1)}, f32[2,512,768]{2,1,0:T(8,128)}, u32[]{:S(2)}) copy-start(f32[2,512,768]{2,1,0:T(8,128)} %copy-done.8) | copy-start | bytes 9437188
  103.4 78.2 %collective-permute-start.9 = (f32[3,256,256]{2,1,0:T(8,128)S(1)}, f32[3,256,256]{2,1,0:T(8,128)S(1)}, u32[]{:S(2)}, u32[]{:S(2)}) collective-permute-start(f32[3,256,256]{2,1,0:T(8,128)S(1)} %get-tuple-element.99), channel_id=1, source_target_pairs={{0,12},{4,8},{8,4},{12,0},{16,28},{20,24},{24,20},{28,16},{1,13},{... | collective-permute-start | bytes 2359304 | tf_op jit(solution)/shard_map/ppermute | solution.py:297
  106.3 75.3 %collective-permute-start.7 = (f32[3,256,256]{2,1,0:T(8,128)S(1)}, f32[3,256,256]{2,1,0:T(8,128)}, u32[]{:S(2)}, u32[]{:S(2)}) collective-permute-start(f32[3,256,256]{2,1,0:T(8,128)S(1)} %get-tuple-element.100), channel_id=1, source_target_pairs={{0,24},{4,28},{8,16},{12,20},{16,8},{20,12},{24,0},{28,4},{1,25},{... | collective-permute-start | bytes 2359304 | tf_op jit(solution)/shard_map/ppermute | solution.py:297
  107.7 84.5 %collective-permute-start.5 = (f32[3,256,256]{2,1,0:T(8,128)S(1)}, f32[3,256,256]{2,1,0:T(8,128)S(1)}, u32[]{:S(2)}, u32[]{:S(2)}) collective-permute-start(f32[3,256,256]{2,1,0:T(8,128)S(1)} %get-tuple-element.101), channel_id=1, source_target_pairs={{0,28},{4,24},{8,20},{12,16},{16,12},{20,8},{24,4},{28,0},{1,29},{... | collective-permute-start | bytes 2359304 | tf_op jit(solution)/shard_map/ppermute | solution.py:297
  107.7 3.5 %copy-start.2 = (f32[2,256,256]{2,1,0:T(8,128)S(1)}, f32[2,256,256]{2,1,0:T(8,128)}, u32[]{:S(2)}) copy-start(f32[2,256,256]{2,1,0:T(8,128)} %refs_1_.1) | copy-start | bytes 1572868
  107.7 3.5 %copy-start.4 = (bf16[2,256,768]{2,1,0:T(8,128)(2,1)S(1)}, bf16[2,256,768]{2,1,0:T(8,128)(2,1)}, u32[]{:S(2)}) copy-start(bf16[2,256,768]{2,1,0:T(8,128)(2,1)} %constant.215.clone.left_ref) | copy-start | bytes 2359300
  107.7 3.5 %copy-start.5 = (bf16[2,768,256]{2,1,0:T(8,128)(2,1)S(1)}, bf16[2,768,256]{2,1,0:T(8,128)(2,1)}, u32[]{:S(2)}) copy-start(bf16[2,768,256]{2,1,0:T(8,128)(2,1)} %constant.213.clone.right_ref) | copy-start | bytes 2359300
  107.7 64.5 %collective-permute-start.10 = (f32[3,256,256]{2,1,0:T(8,128)S(1)}, f32[3,256,256]{2,1,0:T(8,128)S(1)}, u32[]{:S(2)}, u32[]{:S(2)}) collective-permute-start(f32[3,256,256]{2,1,0:T(8,128)S(1)} %get-tuple-element.102), channel_id=1, source_target_pairs={{0,8},{4,12},{8,0},{12,4},{16,24},{20,28},{24,16},{28,20},{1,9},{5... | collective-permute-start | bytes 2359304 | tf_op jit(solution)/shard_map/ppermute | solution.py:297
  111.2 26.2 %copy-start = (bf16[2,256,768]{2,1,0:T(8,128)(2,1)S(1)}, bf16[2,256,768]{2,1,0:T(8,128)(2,1)}, u32[]{:S(2)}) copy-start(bf16[2,256,768]{2,1,0:T(8,128)(2,1)} %constant.216.clone.refs_5_.refs_4_.refs_3_) | copy-start | bytes 2359300
  111.2 26.2 %copy-start.1 = (bf16[2,768,256]{2,1,0:T(8,128)(2,1)S(1)}, bf16[2,768,256]{2,1,0:T(8,128)(2,1)}, u32[]{:S(2)}) copy-start(bf16[2,768,256]{2,1,0:T(8,128)(2,1)} %constant.214.clone.refs_4_.refs_3_.refs_2_) | copy-start | bytes 2359300
  111.2 26.2 %copy-start.3 = (bf16[512,256]{1,0:T(8,128)(2,1)S(1)}, bf16[512,256]{1,0:T(8,128)(2,1)}, u32[]{:S(2)}) copy-start(bf16[512,256]{1,0:T(8,128)(2,1)} %constant.217.clone.refs_6_.refs_5_.refs_4_) | copy-start | bytes 786436
  197.3 16.2 %collective-permute-start.11 = (f32[2,128,512]{2,1,0:T(8,128)S(1)}, f32[2,128,512]{2,1,0:T(8,128)S(1)}, u32[]{:S(2)}, u32[]{:S(2)}) collective-permute-start(f32[2,128,512]{2,1,0:T(8,128)S(1)} %get-tuple-element.109), channel_id=1, source_target_pairs={{0,1},{1,2},{2,3},{4,5},{5,6},{6,7},{8,9},{9,10},{10,11},{12,13},{... | collective-permute-start | bytes 1572872 | tf_op jit(solution)/shard_map/ppermute | solution.py:234
  204.8 36.1 %collective-permute-start.13 = (f32[2,768,128]{2,1,0:T(8,128)S(1)}, f32[2,768,128]{2,1,0:T(8,128)S(1)}, u32[]{:S(2)}, u32[]{:S(2)}) collective-permute-start(f32[2,768,128]{2,1,0:T(8,128)S(1)} %get-tuple-element.107), channel_id=1, source_target_pairs={{0,4},{4,8},{8,12},{12,16},{16,20},{20,24},{24,28},{1,5},{5,9},{9,... | collective-permute-start | bytes 2359304 | tf_op jit(solution)/shard_map/ppermute | solution.py:234
  207.3 36.7 %collective-permute-start.14 = (f32[2,768,128]{2,1,0:T(8,128)S(1)}, f32[2,768,128]{2,1,0:T(8,128)S(1)}, u32[]{:S(2)}, u32[]{:S(2)}) collective-permute-start(f32[2,768,128]{2,1,0:T(8,128)S(1)} %get-tuple-element.106), channel_id=1, source_target_pairs={{4,0},{8,4},{12,8},{16,12},{20,16},{24,20},{28,24},{5,1},{9,5},{13... | collective-permute-start | bytes 2359304 | tf_op jit(solution)/shard_map/ppermute | solution.py:234
  211.2 38.4 %collective-permute-start.12 = (f32[2,128,512]{2,1,0:T(8,128)S(1)}, f32[2,128,512]{2,1,0:T(8,128)S(1)}, u32[]{:S(2)}, u32[]{:S(2)}) collective-permute-start(f32[2,128,512]{2,1,0:T(8,128)S(1)} %get-tuple-element.108), channel_id=1, source_target_pairs={{1,0},{2,1},{3,2},{5,4},{6,5},{7,6},{9,8},{10,9},{11,10},{13,12},{... | collective-permute-start | bytes 1572872 | tf_op jit(solution)/shard_map/ppermute | solution.py:234
  244.1 8.9 %collective-permute-start.16 = (f32[2,128,256]{2,1,0:T(8,128)S(1)}, f32[2,128,256]{2,1,0:T(8,128)S(1)}, u32[]{:S(2)}, u32[]{:S(2)}) collective-permute-start(f32[2,128,256]{2,1,0:T(8,128)S(1)} %get-tuple-element.114), channel_id=1, source_target_pairs={{1,0},{2,1},{3,2},{5,4},{6,5},{7,6},{9,8},{10,9},{11,10},{13,12},{... | collective-permute-start | bytes 786440 | tf_op jit(solution)/shard_map/ppermute | solution.py:234
  246.4 6.6 %collective-permute-start.15 = (f32[2,128,256]{2,1,0:T(8,128)S(1)}, f32[2,128,256]{2,1,0:T(8,128)S(1)}, u32[]{:S(2)}, u32[]{:S(2)}) collective-permute-start(f32[2,128,256]{2,1,0:T(8,128)S(1)} %get-tuple-element.115), channel_id=1, source_target_pairs={{0,1},{1,2},{2,3},{4,5},{5,6},{6,7},{8,9},{9,10},{10,11},{12,13},{... | collective-permute-start | bytes 786440 | tf_op jit(solution)/shard_map/ppermute | solution.py:234
  253.0 1.6 copy-start.7

commit v3 on v2

--- a/solution.py
+++ b/solution.py
@@ -258,8 +258,11 @@
     groups = [group for group in groups if group]
     order = [d for group in groups for d in group]
 
-    before, after = from_sides(object_field[:, :, :half], object_field[:, :, tile - half :], "gx")
-    early = me
+    def chunk_of(d, at):
+        return lax.dynamic_index_in_dim(kept, target_of(d, at), axis=0, keepdims=False)
+
+    leading, sided = lax.optimization_barrier((chunk_of(order[1], me), object_field))
+    before, after = from_sides(sided[:, :, :half], sided[:, :, tile - half :], "gx")
     late, before, after = lax.optimization_barrier((me, before, after))
     field = jnp.concatenate([before, object_field, after], axis=2)
     before, after = from_sides(field[:, :half], field[:, tile - half :], "gy")
@@ -289,11 +292,11 @@
     far = run_forward(info, field, probe, right, left)
     arrived = {}
     for number, d in enumerate(order):
-        at = early if number < 3 else late
+        at = me if d == 0 else late
         if number >= 5:
             past = order[number - 4]
             at, arrived[past] = lax.optimization_barrier((at, arrived[past]))
-        chunk = lax.dynamic_index_in_dim(kept, target_of(d, at), axis=0, keepdims=False)
+        chunk = leading if number == 1 else chunk_of(d, at)
         arrived[d] = chunk if d == 0 else lax.ppermute(chunk, "gx", [(i, target_of(d, i)) for i in ids])
 
     summed, first = None, 0
@@ -303,19 +306,24 @@
         )
         first += len(group) * slots
 
-    west, east = from_sides(summed[:, :, :half], summed[:, :, tile + half :], "gx")
-    inner = summed[:, :, half : half + tile]
-    north, south = from_sides(inner[:, :half], inner[:, tile + half :], "gy")
-    corners = jnp.concatenate([west, east], axis=2)
-    corner_north, corner_south = from_sides(corners[:, :half], corners[:, tile + half :], "gy")
-    gradient = inner[:, half : half + tile]
-    gradient = gradient.at[:, :half].add(north)
-    gradient = gradient.at[:, tile - half :].add(south)
-    side = corners[:, half : half + tile]
-    side = side.at[:, :half].add(corner_north)
-    side = side.at[:, tile - half :].add(corner_south)
-    gradient = gradient.at[:, :, :half].add(side[:, :, :half])
-    gradient = gradient.at[:, :, tile - half :].add(side[:, :, half:])
+    top, middle, bottom = slice(0, half), slice(half, tile - half), slice(tile - half, tile)
+    inner = summed[:, half : half + tile]
+    sent = (
+        summed[:, :half], summed[:, tile + half :], inner[:, middle, :half], inner[:, middle, tile + half :]
+    )
+    sent = lax.optimization_barrier(sent)
+    north, south = from_sides(sent[0], sent[1], "gy")
+    west_mid, east_mid = from_sides(sent[2], sent[3], "gx")
+    north, south, west_mid, east_mid = lax.optimization_barrier((north, south, west_mid, east_mid))
+    upper, lower = inner[:, top] + north, inner[:, bottom] + south
+    ends = jnp.concatenate([upper, lower], axis=1)
+    west_ends, east_ends = from_sides(ends[:, :, :half], ends[:, :, tile + half :], "gx")
+    west = jnp.concatenate([west_ends[:, :half], west_mid, west_ends[:, half:]], axis=1)
+    east = jnp.concatenate([east_ends[:, :half], east_mid, east_ends[:, half:]], axis=1)
+    own = slice(half, half + tile)
+    gradient = jnp.concatenate([upper[:, :, own], inner[:, middle, own], lower[:, :, own]], axis=1)
+    gradient = gradient.at[:, :, :half].add(west)
+    gradient = gradient.at[:, :, tile - half :].add(east)
     return object_field - step_size * (gradient + ridge * object_field)
 
 

time: 258 us -> 233 us (0.903)
  waiting for transfers between devices: 131 us -> 110 us
  Pallas kernels: 64.1 us -> 57.7 us
    ppermute x7, waiting for transfers between devices: 76.5 us -> 50.8 us  [per_device(): lax.ppermute(chunk, 'gx', [(i, target_of(d, i)) for i in ids])]
    ppermute x5, waiting for transfers between devices: 23.4 us -> 42.6 us  [from_sides(): lax.ppermute(low_part, axis, backward)]
    ppermute x5, waiting for transfers between devices: 31.3 us -> 16.6 us  [from_sides(): lax.ppermute(high_part, axis, forward)]
    ppermute x7, starting transfers between devices: 10.6 us -> 5.77 us  [per_device(): lax.ppermute(chunk, 'gx', [(i, target_of(d, i)) for i in ids])]
    ppermute x5, starting transfers between devices: 13.2 us -> 17.7 us  [from_sides(): lax.ppermute(low_part, axis, backward)]
    pallas_call x4, Pallas kernels: 37.9 us -> 34.4 us  [run_backward(): pl.pallas_call(functools.partial(backward_kernel, extent // size, len(fra...]
    pallas_call x1, Pallas kernels: 26.1 us -> 23.3 us  [run_forward(): pl.pallas_call(functools.partial(forward_kernel, field.shape[1] // size),...]
    squeeze x2 -> x3, local copies, waits for them, and re-layouts: 5.83 us -> 7.44 us  [chunk_of(): lax.dynamic_index_in_dim(kept, target_of(d, at), axis=0, keepdims=False)]
  transfers between devices with their start and end apart: 17 -> 17, of which waited for: 9 -> 8; matrix products, arithmetic and copies ran while one was open for 3% -> 5% of each run, Pallas kernels for 23% -> 23%
where the time goes in v3:
time: 233 us; the launch traced here: 231 us
  waiting for transfers between devices  110 us (47%)
  Pallas kernels  57.7 us (25%)
  starting transfers between devices  43.2 us (19%)
  local copies, waits for them, and re-layouts  14.2 us (6%)
  other arithmetic  4.39 us (2%)
    ppermute x7, waiting for transfers between devices, per_device(): lax.ppermute(chunk, 'gx', [(i, target_of(d, i)) for i in ids])  50.8 us
    ppermute x5, waiting for transfers between devices, from_sides(): lax.ppermute(low_part, axis, backward)  42.6 us
    pallas_call x4, Pallas kernels, run_backward(): pl.pallas_call(functools.partial(backward_kernel, extent // size, len(fra...  34.4 us
    pallas_call x1, Pallas kernels, run_forward(): pl.pallas_call(functools.partial(forward_kernel, field.shape[1] // size),...  23.3 us
    ppermute x5, starting transfers between devices, from_sides(): lax.ppermute(high_part, axis, forward)  19.8 us
    ppermute x5, starting transfers between devices, from_sides(): lax.ppermute(low_part, axis, backward)  17.7 us
    ppermute x5, waiting for transfers between devices, from_sides(): lax.ppermute(high_part, axis, forward)  16.6 us
    squeeze x3, local copies, waits for them, and re-layouts, chunk_of(): lax.dynamic_index_in_dim(kept, target_of(d, at), axis=0, keepdims=False)  7.44 us
  transfers between devices with their start and end apart: 17, of which 8 were waited for; matrix products, arithmetic and copies ran while one was open for 5% of the time, Pallas kernels for 23%

profile of v3, /device:TPU:17, one launch (start us, length us, event | category | flops | bytes accessed | tf_op | source)
XLA Modules:
  0.0 230.6 jit_solution(14064796828054538437)
XLA Ops:
  0.0 2.1 dynamic-slice_bitcast_fusion.7
  2.1 0.0 collective-permute-start.6
  2.1 1.3 fusion.6
  3.4 5.3 %collective-permute-start.1 = (f32[2,512,128]{2,1,0:T(8,128)S(1)}, f32[2,512,128]{2,1,0:T(8,128)S(1)}, u32[]{:S(2)}, u32[]{:S(2)}) collective-permute-start(f32[2,512,128]{2,1,0:T(8,128)S(1)} %get-tuple-element.85), channel_id=1, source_target_pairs={{4,0},{8,4},{12,8},{16,12},{20,16},{24,20},{28,24},{5,1},{9,5},{13... | collective-permute-start | bytes 1572872 | tf_op jit(solution)/shard_map/ppermute | solution.py:234
  8.7 1.9 collective-permute-start
  10.7 0.2 convert_reduce_fusion.1
  11.0 36.0 %collective-permute-done.1 = f32[2,512,128]{2,1,0:T(8,128)S(1)} collective-permute-done((f32[2,512,128]{2,1,0:T(8,128)S(1)}, f32[2,512,128]{2,1,0:T(8,128)S(1)}, u32[]{:S(2)}, u32[]{:S(2)}) %collective-permute-start.1) | collective-permute-done | bytes 524320 | tf_op jit(solution)/shard_map/ppermute | solution.py:234
  46.9 4.8 %collective-permute-done = f32[2,512,128]{2,1,0:T(8,128)S(1)} collective-permute-done((f32[2,512,128]{2,1,0:T(8,128)S(1)}, f32[2,512,128]{2,1,0:T(8,128)S(1)}, u32[]{:S(2)}, u32[]{:S(2)}) %collective-permute-start) | collective-permute-done | bytes 524320 | tf_op jit(solution)/shard_map/ppermute | solution.py:234
  51.7 2.8 %dynamic-slice_bitcast_fusion.3 = (f32[3,256,256]{2,1,0:T(8,128)}, f32[3,256,256]{2,1,0:T(8,128)}) fusion(f32[1,1,8,3,256,256]{5,4,3,2,1,0:T(8,128)} %param.17, s32[]{:T(128)S(6)} %select_n.29, s32[]{:T(128)S(6)} %select_n.26), kind=kLoop, calls=%fused_computation.8 | loop fusion | bytes 3145736 | tf_op jit(solution)/shard_map/jit(dynamic_index_in_dim)/squeeze | solution.py:262
  54.5 0.0 collective-permute-start.8
  54.5 0.0 collective-permute-start.4
  54.5 1.8 constant_dynamic-update-slice_fusion.1
  56.4 1.6 copy-done.7
  58.0 1.3 fusion.5
  59.3 3.5 %collective-permute-start.2 = (f32[2,128,768]{2,1,0:T(8,128)}, f32[2,128,768]{2,1,0:T(8,128)S(1)}, u32[]{:S(2)}, u32[]{:S(2)}) collective-permute-start(f32[2,128,768]{2,1,0:T(8,128)} %get-tuple-element.83), channel_id=1, source_target_pairs={{0,1},{1,2},{2,3},{4,5},{5,6},{6,7},{8,9},{9,10},{10,11},{12,13},{... | collective-permute-start | bytes 2359304 | tf_op jit(solution)/shard_map/ppermute | solution.py:234
  62.8 1.9 collective-permute-start.3
  65.3 0.1 concatenate.25
  65.4 0.2 select_reduce_fusion.1
  65.7 0.1 slice.131.info_ref
  65.7 0.1 fusion.9
  65.8 0.0 collective-permute-done.6.refs_1_
  65.8 24.3 %collective-permute-done.8.refs_2_ = f32[3,256,256]{2,1,0:T(8,128)S(1)} collective-permute-done((f32[3,256,256]{2,1,0:T(8,128)}, f32[3,256,256]{2,1,0:T(8,128)S(1)}, u32[]{:S(2)}, u32[]{:S(2)}) %collective-permute-start.8) | collective-permute-done | bytes 786464 | tf_op jit(solution)/shard_map/ppermute | solution.py:300
  90.2 0.0 collective-permute-done.4.refs_0_
  90.2 2.6 %dynamic-slice_bitcast_fusion = (f32[3,256,256]{2,1,0:T(8,128)S(1)}, f32[3,256,256]{2,1,0:T(8,128)S(1)}, f32[3,256,256]{2,1,0:T(8,128)S(1)}, f32[3,256,256]{2,1,0:T(8,128)S(1)}, f32[3,256,256]{2,1,0:T(8,128)S(1)}) fusion(f32[1,1,8,3,256,256]{5,4,3,2,1,0:T(8,128)} %param.17, s32[]{:T(128)S(6)} %select_n.32, s32[]{:T(128)S(6)} %select_n.30, s32[]{:T(128)S(6)} %select_n.28, ...), kind=kLoop, calls=%fused_computation.5 | loop fusion | bytes 7864340 | tf_op jit(solution)/shard_map/jit(dynamic_index_in_dim)/squeeze | solution.py:262
  92.8 0.2 collective-permute-start.9
  93.0 2.6 %collective-permute-start.7 = (f32[3,256,256]{2,1,0:T(8,128)S(1)}, f32[3,256,256]{2,1,0:T(8,128)}, u32[]{:S(2)}, u32[]{:S(2)}) collective-permute-start(f32[3,256,256]{2,1,0:T(8,128)S(1)} %get-tuple-element.72), channel_id=1, source_target_pairs={{0,24},{4,28},{8,16},{12,20},{16,8},{20,12},{24,0},{28,4},{1,25},{... | collective-permute-start | bytes 2359304 | tf_op jit(solution)/shard_map/ppermute | solution.py:300
  95.6 1.2 collective-permute-start.5
  96.8 0.0 collective-permute-done.2
  96.8 1.7 collective-permute-start.10
  98.5 0.0 collective-permute-done.3
  98.5 1.4 pad_maximum_fusion.field_ref
  100.0 0.0 copy-start
  100.0 0.0 copy-start.1
  100.0 0.0 copy-start.3
  100.1 23.3 %forward.1.far_ref = f32[24,2,256,256]{3,2,1,0:T(8,128)} custom-call(s32[3,24]{1,0:T(4,128)S(1)} %pad_add_fusion.info_ref, f32[2,768,768]{2,1,0:T(8,128)S(1)} %pad_maximum_fusion.field_ref, f32[2,256,256]{2,1,0:T(8,128)S(1)} %copy-done.2, bf16[2,768,256]{2,1,0:T(8,128)(2,1)S(1)} %copy-done.5, bf16[2,256,768]{2,1,0:T(8,128)(2,1)S(1)} %copy-done.4), custom_call_target="tpu_custom_call" | custom-call | flops 9663676416 | bytes 17301504 | tf_op jit(solution)/shard_map/forward/pallas_call | solution.py:183
  123.4 11.7 %backward.4.refs_6_ = f32[2,768,768]{2,1,0:T(8,128)S(1)} custom-call(s32[3,9]{1,0:T(4,128)S(1)} %bitcast.29, f32[24,2,256,256]{3,2,1,0:T(8,128)} %forward.1.far_ref, f32[3,256,256]{2,1,0:T(8,128)S(1)} %get-tuple-element.70.refs_0_, f32[3,256,256]{2,1,0:T(8,128)S(1)} %collective-permute-done.6.refs_1_, f32[3,256,256]{2,1,0:T(8,128)S(1)} %collective-permute-done.8.refs_2_, ...), custom_call_target="tpu_custom_call" | custom-call | flops 3623878656 | bytes 7077888 | tf_op jit(solution)/shard_map/backward/pallas_call | solution.py:210
  135.1 26.4 %collective-permute-done.10.refs_1_ = f32[3,256,256]{2,1,0:T(8,128)S(1)} collective-permute-done((f32[3,256,256]{2,1,0:T(8,128)S(1)}, f32[3,256,256]{2,1,0:T(8,128)S(1)}, u32[]{:S(2)}, u32[]{:S(2)}) %collective-permute-start.10) | collective-permute-done | bytes 786464 | tf_op jit(solution)/shard_map/ppermute | solution.py:300
  161.5 10.4 %backward.5.refs_6_ = f32[2,768,768]{2,1,0:T(8,128)S(1)} custom-call(s32[3,6]{1,0:T(4,128)S(1)} %get-tuple-element.93.info_ref, f32[24,2,256,256]{3,2,1,0:T(8,128)} %forward.1.far_ref, f32[3,256,256]{2,1,0:T(8,128)S(1)} %collective-permute-done.4.refs_0_, f32[3,256,256]{2,1,0:T(8,128)S(1)} %collective-permute-done.10.refs_1_, f32[2,256,256]{2,1,0:T(8,128)S(1)} %copy-done.2, ...), custom_call_target="tpu_custom_call" | custom-call | flops 2415919104 | bytes 4718592 | tf_op jit(solution)/shard_map/backward/pallas_call | solution.py:210
  171.9 0.0 collective-permute-done.9.refs_1_
  171.9 0.0 collective-permute-done.7.refs_0_
  171.9 7.8 %backward.6.refs_5_ = f32[2,768,768]{2,1,0:T(8,128)S(1)} custom-call(s32[3,6]{1,0:T(4,128)S(1)} %get-tuple-element.94.info_ref, f32[24,2,256,256]{3,2,1,0:T(8,128)} %forward.1.far_ref, f32[3,256,256]{2,1,0:T(8,128)} %collective-permute-done.7.refs_0_, f32[3,256,256]{2,1,0:T(8,128)S(1)} %collective-permute-done.9.refs_1_, f32[2,256,256]{2,1,0:T(8,128)S(1)} %copy-done.2, ...), custom_call_target="tpu_custom_call" | custom-call | flops 2415919104 | bytes 4718592 | tf_op jit(solution)/shard_map/backward/pallas_call | solution.py:210
  179.8 0.0 collective-permute-done.5.refs_0_
  179.8 4.5 %backward.7 = f32[2,768,768]{2,1,0:T(8,128)S(1)} custom-call(s32[3,3]{1,0:T(4,128)S(1)} %slice.131.info_ref, f32[24,2,256,256]{3,2,1,0:T(8,128)} %forward.1.far_ref, f32[3,256,256]{2,1,0:T(8,128)S(1)} %collective-permute-done.5.refs_0_, f32[2,256,256]{2,1,0:T(8,128)S(1)} %copy-done.2, bf16[2,768,256]{2,1,0:T(8,128)(2,1)S(1)} %copy-done.1, ...), custom_call_target="tpu_custom_call" | custom-call | flops 1207959552 | bytes 2359296 | tf_op jit(solution)/shard_map/backward/pallas_call | solution.py:210
  184.3 0.1 fusion.4
  184.5 10.5 %collective-permute-start.11 = (f32[2,128,768]{2,1,0:T(8,128)S(1)}, f32[2,128,768]{2,1,0:T(8,128)S(1)}, u32[]{:S(2)}, u32[]{:S(2)}) collective-permute-start(f32[2,128,768]{2,1,0:T(8,128)S(1)} %get-tuple-element.59), channel_id=1, source_target_pairs={{0,1},{1,2},{2,3},{4,5},{5,6},{6,7},{8,9},{9,10},{10,11},{12,13},{... | collective-permute-start | bytes 2359304 | tf_op jit(solution)/shard_map/ppermute | solution.py:234
  195.0 1.9 collective-permute-start.12
  196.9 1.9 collective-permute-start.13
  198.8 4.3 %collective-permute-start.14 = (f32[2,256,128]{2,1,0:T(8,128)S(1)}, f32[2,256,128]{2,1,0:T(8,128)S(1)}, u32[]{:S(2)}, u32[]{:S(2)}) collective-permute-start(f32[2,256,128]{2,1,0:T(8,128)S(1)} %get-tuple-element.62), channel_id=1, source_target_pairs={{4,0},{8,4},{12,8},{16,12},{20,16},{24,20},{28,24},{5,1},{9,5},{13... | collective-permute-start | bytes 786440 | tf_op jit(solution)/shard_map/ppermute | solution.py:234
  203.1 5.3 %collective-permute-done.13 = f32[2,256,128]{2,1,0:T(8,128)S(1)} collective-permute-done((f32[2,256,128]{2,1,0:T(8,128)S(1)}, f32[2,256,128]{2,1,0:T(8,128)S(1)}, u32[]{:S(2)}, u32[]{:S(2)}) %collective-permute-start.13) | collective-permute-done | bytes 262176 | tf_op jit(solution)/shard_map/ppermute | solution.py:234
  208.4 3.3 %collective-permute-done.14 = f32[2,256,128]{2,1,0:T(8,128)S(1)} collective-permute-done((f32[2,256,128]{2,1,0:T(8,128)S(1)}, f32[2,256,128]{2,1,0:T(8,128)S(1)}, u32[]{:S(2)}, u32[]{:S(2)}) %collective-permute-start.14) | collective-permute-done | bytes 262176 | tf_op jit(solution)/shard_map/ppermute | solution.py:234
  211.7 0.0 collective-permute-done.12
  211.7 0.2 slice_add_fusion.1
  212.0 1.9 collective-permute-start.15
  213.9 0.1 slice.164
  214.0 0.1 slice.163
  214.1 0.1 slice.166
  214.2 4.3 %collective-permute-start.16 = (f32[2,256,128]{2,1,0:T(8,128)S(1)}, f32[2,256,128]{2,1,0:T(8,128)S(1)}, u32[]{:S(2)}, u32[]{:S(2)}) collective-permute-start(f32[2,256,128]{2,1,0:T(8,128)S(1)} %get-tuple-element.87), channel_id=1, source_target_pairs={{4,0},{8,4},{12,8},{16,12},{20,16},{24,20},{28,24},{5,1},{9,5},{13... | collective-permute-start | bytes 786440 | tf_op jit(solution)/shard_map/ppermute | solution.py:234
  218.4 0.2 pad_maximum_fusion.1
  218.6 0.0 copy-start.6
  218.6 6.5 %collective-permute-done.15 = f32[2,256,128]{2,1,0:T(8,128)S(1)} collective-permute-done((f32[2,256,128]{2,1,0:T(8,128)S(1)}, f32[2,256,128]{2,1,0:T(8,128)S(1)}, u32[]{:S(2)}, u32[]{:S(2)}) %collective-permute-start.15) | collective-permute-done | bytes 262176 | tf_op jit(solution)/shard_map/ppermute | solution.py:234
  225.1 0.1 fusion.1
  225.3 3.4 %collective-permute-done.16 = f32[2,256,128]{2,1,0:T(8,128)S(1)} collective-permute-done((f32[2,256,128]{2,1,0:T(8,128)S(1)}, f32[2,256,128]{2,1,0:T(8,128)S(1)}, u32[]{:S(2)}, u32[]{:S(2)}) %collective-permute-start.16) | collective-permute-done | bytes 262176 | tf_op jit(solution)/shard_map/ppermute | solution.py:234
  228.6 0.1 fusion
  228.8 1.8 multiply_subtract_fusion
  (33 shorter events, 0.3 us)
Async XLA Ops:
  0.0 10.7 %copy-start.10 = (s32[1,1,24,1]{2,3,1,0:T(1,128)S(1)}, s32[1,1,24,1]{2,3,1,0:T(1,128)}, u32[]{:S(2)}) copy-start(s32[1,1,24,1]{2,3,1,0:T(1,128)} %param.19) | copy-start | bytes 292
  0.0 10.9 %copy-start.9 = (s32[1,1,24,2]{2,3,1,0:T(2,128)S(1)}, s32[1,1,24,2]{2,3,1,0:T(2,128)}, u32[]{:S(2)}) copy-start(s32[1,1,24,2]{2,3,1,0:T(2,128)} %param.18) | copy-start | bytes 580
  2.1 63.7 %collective-permute-start.6 = (f32[3,256,256]{2,1,0:T(8,128)}, f32[3,256,256]{2,1,0:T(8,128)S(1)}, u32[]{:S(2)}, u32[]{:S(2)}) collective-permute-start(f32[3,256,256]{2,1,0:T(8,128)} %dynamic-slice_bitcast_fusion.7), channel_id=1, source_target_pairs={{0,16},{4,20},{8,24},{12,28},{16,0},{20,4},{24,8},{28,12},{1,17},{... | collective-permute-start | bytes 2359304 | tf_op jit(solution)/shard_map/ppermute | solution.py:300
  3.4 43.5 %collective-permute-start.1 = (f32[2,512,128]{2,1,0:T(8,128)S(1)}, f32[2,512,128]{2,1,0:T(8,128)S(1)}, u32[]{:S(2)}, u32[]{:S(2)}) collective-permute-start(f32[2,512,128]{2,1,0:T(8,128)S(1)} %get-tuple-element.85), channel_id=1, source_target_pairs={{4,0},{8,4},{12,8},{16,12},{20,16},{24,20},{28,24},{5,1},{9,5},{13... | collective-permute-start | bytes 1572872 | tf_op jit(solution)/shard_map/ppermute | solution.py:234
  8.7 43.0 %collective-permute-start = (f32[2,512,128]{2,1,0:T(8,128)S(1)}, f32[2,512,128]{2,1,0:T(8,128)S(1)}, u32[]{:S(2)}, u32[]{:S(2)}) collective-permute-start(f32[2,512,128]{2,1,0:T(8,128)S(1)} %get-tuple-element.86), channel_id=1, source_target_pairs={{0,4},{4,8},{8,12},{12,16},{16,20},{20,24},{24,28},{1,5},{5,9},{9,... | collective-permute-start | bytes 1572872 | tf_op jit(solution)/shard_map/ppermute | solution.py:234
  54.5 35.7 %collective-permute-start.8 = (f32[3,256,256]{2,1,0:T(8,128)}, f32[3,256,256]{2,1,0:T(8,128)S(1)}, u32[]{:S(2)}, u32[]{:S(2)}) collective-permute-start(f32[3,256,256]{2,1,0:T(8,128)} %get-tuple-element.75), channel_id=1, source_target_pairs={{0,4},{4,0},{8,12},{12,8},{16,20},{20,16},{24,28},{28,24},{1,5},{5... | collective-permute-start | bytes 2359304 | tf_op jit(solution)/shard_map/ppermute | solution.py:300
  54.5 35.7 %collective-permute-start.4 = (f32[3,256,256]{2,1,0:T(8,128)}, f32[3,256,256]{2,1,0:T(8,128)S(1)}, u32[]{:S(2)}, u32[]{:S(2)}) collective-permute-start(f32[3,256,256]{2,1,0:T(8,128)} %get-tuple-element.76), channel_id=1, source_target_pairs={{0,20},{4,16},{8,28},{12,24},{16,4},{20,0},{24,12},{28,8},{1,21},{... | collective-permute-start | bytes 2359304 | tf_op jit(solution)/shard_map/ppermute | solution.py:300
  56.3 1.6 copy-start.7
  59.3 37.5 %collective-permute-start.2 = (f32[2,128,768]{2,1,0:T(8,128)}, f32[2,128,768]{2,1,0:T(8,128)S(1)}, u32[]{:S(2)}, u32[]{:S(2)}) collective-permute-start(f32[2,128,768]{2,1,0:T(8,128)} %get-tuple-element.83), channel_id=1, source_target_pairs={{0,1},{1,2},{2,3},{4,5},{5,6},{6,7},{8,9},{9,10},{10,11},{12,13},{... | collective-permute-start | bytes 2359304 | tf_op jit(solution)/shard_map/ppermute | solution.py:234
  62.8 35.8 %collective-permute-start.3 = (f32[2,128,768]{2,1,0:T(8,128)}, f32[2,128,768]{2,1,0:T(8,128)}, u32[]{:S(2)}, u32[]{:S(2)}) collective-permute-start(f32[2,128,768]{2,1,0:T(8,128)} %get-tuple-element.84), channel_id=1, source_target_pairs={{1,0},{2,1},{3,2},{5,4},{6,5},{7,6},{9,8},{10,9},{11,10},{13,12},{... | collective-permute-start | bytes 2359304 | tf_op jit(solution)/shard_map/ppermute | solution.py:234
  90.2 8.4 %copy-start.8 = (f32[2,512,768]{2,1,0:T(8,128)S(1)}, f32[2,512,768]{2,1,0:T(8,128)}, u32[]{:S(2)}) copy-start(f32[2,512,768]{2,1,0:T(8,128)} %copy-done.7) | copy-start | bytes 9437188
  92.8 79.1 %collective-permute-start.9 = (f32[3,256,256]{2,1,0:T(8,128)S(1)}, f32[3,256,256]{2,1,0:T(8,128)S(1)}, u32[]{:S(2)}, u32[]{:S(2)}) collective-permute-start(f32[3,256,256]{2,1,0:T(8,128)S(1)} %get-tuple-element.71), channel_id=1, source_target_pairs={{0,12},{4,8},{8,4},{12,0},{16,28},{20,24},{24,20},{28,16},{1,13},{... | collective-permute-start | bytes 2359304 | tf_op jit(solution)/shard_map/ppermute | solution.py:300
  93.0 78.9 %collective-permute-start.7 = (f32[3,256,256]{2,1,0:T(8,128)S(1)}, f32[3,256,256]{2,1,0:T(8,128)}, u32[]{:S(2)}, u32[]{:S(2)}) collective-permute-start(f32[3,256,256]{2,1,0:T(8,128)S(1)} %get-tuple-element.72), channel_id=1, source_target_pairs={{0,24},{4,28},{8,16},{12,20},{16,8},{20,12},{24,0},{28,4},{1,25},{... | collective-permute-start | bytes 2359304 | tf_op jit(solution)/shard_map/ppermute | solution.py:300
  95.6 84.2 %collective-permute-start.5 = (f32[3,256,256]{2,1,0:T(8,128)S(1)}, f32[3,256,256]{2,1,0:T(8,128)S(1)}, u32[]{:S(2)}, u32[]{:S(2)}) collective-permute-start(f32[3,256,256]{2,1,0:T(8,128)S(1)} %get-tuple-element.73), channel_id=1, source_target_pairs={{0,28},{4,24},{8,20},{12,16},{16,12},{20,8},{24,4},{28,0},{1,29},{... | collective-permute-start | bytes 2359304 | tf_op jit(solution)/shard_map/ppermute | solution.py:300
  96.8 3.2 %copy-start.2 = (f32[2,256,256]{2,1,0:T(8,128)S(1)}, f32[2,256,256]{2,1,0:T(8,128)}, u32[]{:S(2)}) copy-start(f32[2,256,256]{2,1,0:T(8,128)} %refs_1_.1) | copy-start | bytes 1572868
  96.8 3.2 %copy-start.4 = (bf16[2,256,768]{2,1,0:T(8,128)(2,1)S(1)}, bf16[2,256,768]{2,1,0:T(8,128)(2,1)}, u32[]{:S(2)}) copy-start(bf16[2,256,768]{2,1,0:T(8,128)(2,1)} %constant.124.clone.left_ref) | copy-start | bytes 2359300
  96.8 3.2 %copy-start.5 = (bf16[2,768,256]{2,1,0:T(8,128)(2,1)S(1)}, bf16[2,768,256]{2,1,0:T(8,128)(2,1)}, u32[]{:S(2)}) copy-start(bf16[2,768,256]{2,1,0:T(8,128)(2,1)} %constant.122.clone.right_ref) | copy-start | bytes 2359300
  96.8 64.7 %collective-permute-start.10 = (f32[3,256,256]{2,1,0:T(8,128)S(1)}, f32[3,256,256]{2,1,0:T(8,128)S(1)}, u32[]{:S(2)}, u32[]{:S(2)}) collective-permute-start(f32[3,256,256]{2,1,0:T(8,128)S(1)} %get-tuple-element.74), channel_id=1, source_target_pairs={{0,8},{4,12},{8,0},{12,4},{16,24},{20,28},{24,16},{28,20},{1,9},{5... | collective-permute-start | bytes 2359304 | tf_op jit(solution)/shard_map/ppermute | solution.py:300
  100.0 23.3 %copy-start = (bf16[2,256,768]{2,1,0:T(8,128)(2,1)S(1)}, bf16[2,256,768]{2,1,0:T(8,128)(2,1)}, u32[]{:S(2)}) copy-start(bf16[2,256,768]{2,1,0:T(8,128)(2,1)} %constant.125.clone.refs_5_.refs_4_.refs_3_) | copy-start | bytes 2359300
  100.0 23.3 %copy-start.1 = (bf16[2,768,256]{2,1,0:T(8,128)(2,1)S(1)}, bf16[2,768,256]{2,1,0:T(8,128)(2,1)}, u32[]{:S(2)}) copy-start(bf16[2,768,256]{2,1,0:T(8,128)(2,1)} %constant.123.clone.refs_4_.refs_3_.refs_2_) | copy-start | bytes 2359300
  100.0 23.3 %copy-start.3 = (bf16[512,256]{1,0:T(8,128)(2,1)S(1)}, bf16[512,256]{1,0:T(8,128)(2,1)}, u32[]{:S(2)}) copy-start(bf16[512,256]{1,0:T(8,128)(2,1)} %constant.126.clone.refs_6_.refs_5_.refs_4_) | copy-start | bytes 786436
  184.5 27.3 %collective-permute-start.11 = (f32[2,128,768]{2,1,0:T(8,128)S(1)}, f32[2,128,768]{2,1,0:T(8,128)S(1)}, u32[]{:S(2)}, u32[]{:S(2)}) collective-permute-start(f32[2,128,768]{2,1,0:T(8,128)S(1)} %get-tuple-element.59), channel_id=1, source_target_pairs={{0,1},{1,2},{2,3},{4,5},{5,6},{6,7},{8,9},{9,10},{10,11},{12,13},{... | collective-permute-start | bytes 2359304 | tf_op jit(solution)/shard_map/ppermute | solution.py:234
  195.0 16.7 %collective-permute-start.12 = (f32[2,128,768]{2,1,0:T(8,128)S(1)}, f32[2,128,768]{2,1,0:T(8,128)S(1)}, u32[]{:S(2)}, u32[]{:S(2)}) collective-permute-start(f32[2,128,768]{2,1,0:T(8,128)S(1)} %get-tuple-element.60), channel_id=1, source_target_pairs={{1,0},{2,1},{3,2},{5,4},{6,5},{7,6},{9,8},{10,9},{11,10},{13,12},{... | collective-permute-start | bytes 2359304 | tf_op jit(solution)/shard_map/ppermute | solution.py:234
  196.9 11.5 %collective-permute-start.13 = (f32[2,256,128]{2,1,0:T(8,128)S(1)}, f32[2,256,128]{2,1,0:T(8,128)S(1)}, u32[]{:S(2)}, u32[]{:S(2)}) collective-permute-start(f32[2,256,128]{2,1,0:T(8,128)S(1)} %get-tuple-element.61), channel_id=1, source_target_pairs={{0,4},{4,8},{8,12},{12,16},{16,20},{20,24},{24,28},{1,5},{5,9},{9,... | collective-permute-start | bytes 786440 | tf_op jit(solution)/shard_map/ppermute | solution.py:234
  198.8 12.9 %collective-permute-start.14 = (f32[2,256,128]{2,1,0:T(8,128)S(1)}, f32[2,256,128]{2,1,0:T(8,128)S(1)}, u32[]{:S(2)}, u32[]{:S(2)}) collective-permute-start(f32[2,256,128]{2,1,0:T(8,128)S(1)} %get-tuple-element.62), channel_id=1, source_target_pairs={{4,0},{8,4},{12,8},{16,12},{20,16},{24,20},{28,24},{5,1},{9,5},{13... | collective-permute-start | bytes 786440 | tf_op jit(solution)/shard_map/ppermute | solution.py:234
  212.0 13.1 %collective-permute-start.15 = (f32[2,256,128]{2,1,0:T(8,128)S(1)}, f32[2,256,128]{2,1,0:T(8,128)S(1)}, u32[]{:S(2)}, u32[]{:S(2)}) collective-permute-start(f32[2,256,128]{2,1,0:T(8,128)S(1)} %get-tuple-element.88), channel_id=1, source_target_pairs={{0,4},{4,8},{8,12},{12,16},{16,20},{20,24},{24,28},{1,5},{5,9},{9,... | collective-permute-start | bytes 786440 | tf_op jit(solution)/shard_map/ppermute | solution.py:234
  214.2 14.5 %collective-permute-start.16 = (f32[2,256,128]{2,1,0:T(8,128)S(1)}, f32[2,256,128]{2,1,0:T(8,128)S(1)}, u32[]{:S(2)}, u32[]{:S(2)}) collective-permute-start(f32[2,256,128]{2,1,0:T(8,128)S(1)} %get-tuple-element.87), channel_id=1, source_target_pairs={{4,0},{8,4},{12,8},{16,12},{20,16},{24,20},{28,24},{5,1},{9,5},{13... | collective-permute-start | bytes 786440 | tf_op jit(solution)/shard_map/ppermute | solution.py:234
  218.6 10.2 %copy-start.6 = (f32[2,512,512]{2,1,0:T(8,128)S(1)}, f32[2,512,512]{2,1,0:T(8,128)}, u32[]{:S(2)}) copy-start(f32[2,512,512]{2,1,0:T(8,128)} %param.15) | copy-start | bytes 6291460

commit v4 on v3

--- a/solution.py
+++ b/solution.py
@@ -251,17 +251,17 @@
         return i ^ d if paired else (i - d + sources) % sources
 
     far_steps, near_steps = ids[sources // 2 :], ids[1 : sources // 2]
-    order = []
-    for number, d in enumerate(far_steps):
-        order += [d] + near_steps[number : number + 1]
-    groups = [[0] + order[:2]] + [order[i : i + 2] for i in range(2, len(order), 2)]
-    groups = [group for group in groups if group]
+    tail = far_steps[2:]
+    groups = [[0] + far_steps[:2] + near_steps[:1]]
+    for steps in (near_steps[1:], tail[:-1], tail[-1:]):
+        groups += [steps[i : i + 2] for i in range(0, len(steps), 2)]
     order = [d for group in groups for d in group]
 
     def chunk_of(d, at):
         return lax.dynamic_index_in_dim(kept, target_of(d, at), axis=0, keepdims=False)
 
-    leading, sided = lax.optimization_barrier((chunk_of(order[1], me), object_field))
+    leading = {d: chunk_of(d, me) for d in far_steps[:2]}
+    leading, sided = lax.optimization_barrier((leading, object_field))
     before, after = from_sides(sided[:, :, :half], sided[:, :, tile - half :], "gx")
     late, before, after = lax.optimization_barrier((me, before, after))
     field = jnp.concatenate([before, object_field, after], axis=2)
@@ -291,12 +291,12 @@
     right, right_t, left, left_t, perm = (jnp.asarray(t) for t in dft_tables(size))
     far = run_forward(info, field, probe, right, left)
     arrived = {}
-    for number, d in enumerate(order):
+    for d in order:
         at = me if d == 0 else late
-        if number >= 5:
-            past = order[number - 4]
+        if d in tail:
+            past = far_steps[far_steps.index(d) - 2]
             at, arrived[past] = lax.optimization_barrier((at, arrived[past]))
-        chunk = leading if number == 1 else chunk_of(d, at)
+        chunk = leading[d] if d in leading else chunk_of(d, at)
         arrived[d] = chunk if d == 0 else lax.ppermute(chunk, "gx", [(i, target_of(d, i)) for i in ids])
 
     summed, first = None, 0

time: 233 us -> 229 us (0.983)
  waiting for transfers between devices: 110 us -> 86.9 us
  starting transfers between devices: 43.2 us -> 65.2 us
  Pallas kernels: 57.7 us -> 55.1 us
    ppermute x5, waiting for transfers between devices: 42.6 us -> 9.54 us  [from_sides(): lax.ppermute(low_part, axis, backward)]
    ppermute x5, waiting for transfers between devices: 16.6 us -> 45.9 us  [from_sides(): lax.ppermute(high_part, axis, forward)]
    ppermute x7, waiting for transfers between devices: 50.8 us -> 31.4 us  [per_device(): lax.ppermute(chunk, 'gx', [(i, target_of(d, i)) for i in ids])]
    ppermute x5, starting transfers between devices: 19.8 us -> 38.1 us  [from_sides(): lax.ppermute(high_part, axis, forward)]
    unnamed x24 -> x38, local copies, waits for them, and re-layouts: 3.48 us -> 4.96 us
    squeeze x3 -> x2, local copies, waits for them, and re-layouts: 7.44 us -> 7.06 us  [chunk_of(): lax.dynamic_index_in_dim(kept, target_of(d, at), axis=0, keepdims=False)]
  transfers between devices with their start and end apart: 17 -> 17, of which waited for: 8 -> 9; matrix products, arithmetic and copies ran while one was open for 5% -> 4% of each run, Pallas kernels for 23% -> 23%
where the time goes in v4:
time: 229 us; the launch traced here: 226 us
  waiting for transfers between devices  86.9 us (38%)
  starting transfers between devices  65.2 us (28%)
  Pallas kernels  55.1 us (24%)
  local copies, waits for them, and re-layouts  15 us (7%)
  other arithmetic  3.25 us (1%)
    ppermute x5, waiting for transfers between devices, from_sides(): lax.ppermute(high_part, axis, forward)  45.9 us
    ppermute x5, starting transfers between devices, from_sides(): lax.ppermute(high_part, axis, forward)  38.1 us
    pallas_call x4, Pallas kernels, run_backward(): pl.pallas_call(functools.partial(backward_kernel, extent // size, len(fra...  33.2 us
    ppermute x7, waiting for transfers between devices, per_device(): lax.ppermute(chunk, 'gx', [(i, target_of(d, i)) for i in ids])  31.4 us
    pallas_call x1, Pallas kernels, run_forward(): pl.pallas_call(functools.partial(forward_kernel, field.shape[1] // size),...  21.8 us
    ppermute x5, starting transfers between devices, from_sides(): lax.ppermute(low_part, axis, backward)  19.9 us
    ppermute x5, waiting for transfers between devices, from_sides(): lax.ppermute(low_part, axis, backward)  9.54 us
    ppermute x7, starting transfers between devices, per_device(): lax.ppermute(chunk, 'gx', [(i, target_of(d, i)) for i in ids])  7.11 us
  transfers between devices with their start and end apart: 17, of which 9 were waited for; matrix products, arithmetic and copies ran while one was open for 4% of the time, Pallas kernels for 23%

profile of v4, /device:TPU:17, one launch (start us, length us, event | category | flops | bytes accessed | tf_op | source)
XLA Modules:
  0.0 226.4 jit_solution(6990690318280679817)
XLA Ops:
  0.0 2.9 %dynamic-slice_bitcast_fusion.6 = (f32[3,256,256]{2,1,0:T(8,128)}, f32[3,256,256]{2,1,0:T(8,128)}) fusion(f32[1,1,8,3,256,256]{5,4,3,2,1,0:T(8,128)} %param.17, s32[]{:T(128)S(6)} %select_n.26, s32[]{:T(128)S(6)} %select_n.25), kind=kLoop, calls=%fused_computation.11 | loop fusion | bytes 3145736 | tf_op jit(solution)/shard_map/jit(dynamic_index_in_dim)/squeeze | solution.py:261
  2.9 0.9 fusion.6
  3.8 3.1 %collective-permute-start = (f32[2,512,128]{2,1,0:T(8,128)}, f32[2,512,128]{2,1,0:T(8,128)S(1)}, u32[]{:S(2)}, u32[]{:S(2)}) collective-permute-start(f32[2,512,128]{2,1,0:T(8,128)} %get-tuple-element.85), channel_id=1, source_target_pairs={{0,4},{4,8},{8,12},{12,16},{16,20},{20,24},{24,28},{1,5},{5,9},{9,... | collective-permute-start | bytes 1572872 | tf_op jit(solution)/shard_map/ppermute | solution.py:234
  6.9 3.0 %collective-permute-start.1 = (f32[2,512,128]{2,1,0:T(8,128)S(1)}, f32[2,512,128]{2,1,0:T(8,128)S(1)}, u32[]{:S(2)}, u32[]{:S(2)}) collective-permute-start(f32[2,512,128]{2,1,0:T(8,128)S(1)} %get-tuple-element.84), channel_id=1, source_target_pairs={{4,0},{8,4},{12,8},{16,12},{20,16},{24,20},{28,24},{5,1},{9,5},{13... | collective-permute-start | bytes 1572872 | tf_op jit(solution)/shard_map/ppermute | solution.py:234
  9.9 0.2 collective-permute-start.4
  10.1 2.3 %collective-permute-start.6 = (f32[3,256,256]{2,1,0:T(8,128)}, f32[3,256,256]{2,1,0:T(8,128)S(1)}, u32[]{:S(2)}, u32[]{:S(2)}) collective-permute-start(f32[3,256,256]{2,1,0:T(8,128)} %get-tuple-element.53), channel_id=1, source_target_pairs={{0,16},{4,20},{8,24},{12,28},{16,0},{20,4},{24,8},{28,12},{1,17},{... | collective-permute-start | bytes 2359304 | tf_op jit(solution)/shard_map/ppermute | solution.py:300
  13.1 0.1 concatenate.25
  13.2 0.2 convert_reduce_fusion.1
  13.4 32.4 %collective-permute-done = f32[2,512,128]{2,1,0:T(8,128)S(1)} collective-permute-done((f32[2,512,128]{2,1,0:T(8,128)}, f32[2,512,128]{2,1,0:T(8,128)S(1)}, u32[]{:S(2)}, u32[]{:S(2)}) %collective-permute-start) | collective-permute-done | bytes 524320 | tf_op jit(solution)/shard_map/ppermute | solution.py:234
  45.9 2.8 %collective-permute-done.1 = f32[2,512,128]{2,1,0:T(8,128)S(1)} collective-permute-done((f32[2,512,128]{2,1,0:T(8,128)S(1)}, f32[2,512,128]{2,1,0:T(8,128)S(1)}, u32[]{:S(2)}, u32[]{:S(2)}) %collective-permute-start.1) | collective-permute-done | bytes 524320 | tf_op jit(solution)/shard_map/ppermute | solution.py:234
  48.7 1.8 constant_dynamic-update-slice_fusion.1
  50.5 1.4 fusion.5
  51.9 3.5 %collective-permute-start.2 = (f32[2,128,768]{2,1,0:T(8,128)}, f32[2,128,768]{2,1,0:T(8,128)S(1)}, u32[]{:S(2)}, u32[]{:S(2)}) collective-permute-start(f32[2,128,768]{2,1,0:T(8,128)} %get-tuple-element.82), channel_id=1, source_target_pairs={{0,1},{1,2},{2,3},{4,5},{5,6},{6,7},{8,9},{9,10},{10,11},{12,13},{... | collective-permute-start | bytes 2359304 | tf_op jit(solution)/shard_map/ppermute | solution.py:234
  55.4 1.9 collective-permute-start.3
  57.4 0.2 select_reduce_fusion.1
  57.6 0.1 slice.137.info_ref
  57.7 0.1 fusion.9
  57.8 13.2 %collective-permute-done.4.refs_2_ = f32[3,256,256]{2,1,0:T(8,128)S(1)} collective-permute-done((f32[3,256,256]{2,1,0:T(8,128)}, f32[3,256,256]{2,1,0:T(8,128)S(1)}, u32[]{:S(2)}, u32[]{:S(2)}) %collective-permute-start.4) | collective-permute-done | bytes 786464 | tf_op jit(solution)/shard_map/ppermute | solution.py:300
  70.9 16.9 %collective-permute-done.6.refs_1_ = f32[3,256,256]{2,1,0:T(8,128)S(1)} collective-permute-done((f32[3,256,256]{2,1,0:T(8,128)}, f32[3,256,256]{2,1,0:T(8,128)S(1)}, u32[]{:S(2)}, u32[]{:S(2)}) %collective-permute-start.6) | collective-permute-done | bytes 786464 | tf_op jit(solution)/shard_map/ppermute | solution.py:300
  87.8 4.2 %dynamic-slice_bitcast_fusion = (f32[3,256,256]{2,1,0:T(8,128)S(1)}, f32[3,256,256]{2,1,0:T(8,128)S(1)}, f32[3,256,256]{2,1,0:T(8,128)S(1)}, f32[3,256,256]{2,1,...) fusion(f32[1,1,8,3,256,256]{5,4,3,2,1,0:T(8,128)} %param.17, s32[]{:T(128)S(6)} %select_n.32, ...), kind=kLoop, calls=%fused_computation.5 | loop fusion | bytes 9437208 | tf_op jit(solution)/shard_map/jit(dynamic_index_in_dim)/squeeze | solution.py:261
  92.0 0.1 collective-permute-start.10
  92.1 0.7 collective-permute-start.8
  92.8 1.9 collective-permute-start.9
  94.7 0.0 collective-permute-done.2
  94.7 1.8 collective-permute-start.7
  96.5 0.0 collective-permute-done.3
  96.6 0.1 collective-permute-start.5
  96.7 0.3 pad_maximum_fusion.field_ref
  97.0 0.6 copy-done.2
  97.6 0.3 copy-done.10
  97.8 0.2 copy-done.11
  98.1 21.8 %forward.1.far_ref = f32[24,2,256,256]{3,2,1,0:T(8,128)} custom-call(s32[3,24]{1,0:T(4,128)S(1)} %pad_add_fusion.info_ref, f32[2,768,768]{2,1,0:T(8,128)S(1)} %pad_maximum_fusion.field_ref, f32[2,256,256]{2,1,0:T(8,128)S(1)} %copy-done.2, bf16[2,768,256]{2,1,0:T(8,128)(2,1)S(1)} %copy-done.10, bf16[2,256,768]{2,1,0:T(8,128)(2,1)S(1)} %copy-done.11), custom_call_target="tpu_custom_call" | custom-call | flops 9663676416 | bytes 17301504 | tf_op jit(solution)/shard_map/forward/pallas_call | solution.py:183
  119.9 0.0 collective-permute-done.10.refs_3_
  120.0 16.6 %backward.4.refs_6_ = f32[2,768,768]{2,1,0:T(8,128)S(1)} custom-call(s32[3,12]{1,0:T(4,128)S(1)} %bitcast.29, f32[24,2,256,256]{3,2,1,0:T(8,128)} %forward.1.far_ref, f32[3,256,256]{2,1,0:T(8,128)S(1)} %get-tuple-element.73.refs_0_, f32[3,256,256]{2,1,0:T(8,128)S(1)} %copy-done.7, f32[3,256,256]{2,1,0:T(8,128)S(1)} %copy-done.5, ...), custom_call_target="tpu_custom_call" | custom-call | flops 4831838208 | bytes 9437184 | tf_op jit(solution)/shard_map/backward/pallas_call | solution.py:210
  136.6 1.4 collective-permute-done.9.refs_1_
  138.0 8.5 %backward.5.refs_5_ = f32[2,768,768]{2,1,0:T(8,128)S(1)} custom-call(s32[3,6]{1,0:T(4,128)S(1)} %slice.137.info_ref, f32[24,2,256,256]{3,2,1,0:T(8,128)} %forward.1.far_ref, f32[3,256,256]{2,1,0:T(8,128)S(1)} %collective-permute-done.8.refs_0_, f32[3,256,256]{2,1,0:T(8,128)S(1)} %collective-permute-done.9.refs_1_, f32[2,256,256]{2,1,0:T(8,128)S(1)} %copy-done.2, ...), custom_call_target="tpu_custom_call" | custom-call | flops 2415919104 | bytes 4718592 | tf_op jit(solution)/shard_map/backward/pallas_call | solution.py:210
  146.4 0.0 copy-start.8
  146.5 0.9 copy-done.8
  147.3 1.1 copy-done.9
  148.5 5.0 %backward.6.refs_5_ = f32[2,768,768]{2,1,0:T(8,128)S(1)} custom-call(s32[3,3]{1,0:T(4,128)S(1)} %get-tuple-element.92.info_ref, f32[24,2,256,256]{3,2,1,0:T(8,128)} %forward.1.far_ref, f32[3,256,256]{2,1,0:T(8,128)S(1)} %copy-done.9, f32[2,256,256]{2,1,0:T(8,128)S(1)} %copy-done.2, bf16[2,768,256]{2,1,0:T(8,128)(2,1)S(1)} %copy-done, ...), custom_call_target="tpu_custom_call" | custom-call | flops 1207959552 | bytes 2359296 | tf_op jit(solution)/shard_map/backward/pallas_call | solution.py:210
  153.4 0.0 collective-permute-done.5.refs_0_
  153.4 3.2 %backward.7 = f32[2,768,768]{2,1,0:T(8,128)S(1)} custom-call(s32[3,3]{1,0:T(4,128)S(1)} %get-tuple-element.93.info_ref, f32[24,2,256,256]{3,2,1,0:T(8,128)} %forward.1.far_ref, f32[3,256,256]{2,1,0:T(8,128)} %collective-permute-done.5.refs_0_, f32[2,256,256]{2,1,0:T(8,128)S(1)} %copy-done.2, bf16[2,768,256]{2,1,0:T(8,128)(2,1)S(1)} %copy-done, ...), custom_call_target="tpu_custom_call" | custom-call | flops 1207959552 | bytes 2359296 | tf_op jit(solution)/shard_map/backward/pallas_call | solution.py:210
  156.7 0.1 fusion.4
  156.8 27.7 %collective-permute-start.11 = (f32[2,128,768]{2,1,0:T(8,128)S(1)}, f32[2,128,768]{2,1,0:T(8,128)S(1)}, u32[]{:S(2)}, u32[]{:S(2)}) collective-permute-start(f32[2,128,768]{2,1,0:T(8,128)S(1)} %get-tuple-element.57), channel_id=1, source_target_pairs={{0,1},{1,2},{2,3},{4,5},{5,6},{6,7},{8,9},{9,10},{10,11},{12,13},{... | collective-permute-start | bytes 2359304 | tf_op jit(solution)/shard_map/ppermute | solution.py:234
  184.5 6.4 %collective-permute-start.12 = (f32[2,128,768]{2,1,0:T(8,128)S(1)}, f32[2,128,768]{2,1,0:T(8,128)S(1)}, u32[]{:S(2)}, u32[]{:S(2)}) collective-permute-start(f32[2,128,768]{2,1,0:T(8,128)S(1)} %get-tuple-element.58), channel_id=1, source_target_pairs={{1,0},{2,1},{3,2},{5,4},{6,5},{7,6},{9,8},{10,9},{11,10},{13,12},{... | collective-permute-start | bytes 2359304 | tf_op jit(solution)/shard_map/ppermute | solution.py:234
  191.0 1.9 collective-permute-start.13
  192.9 4.3 %collective-permute-start.14 = (f32[2,256,128]{2,1,0:T(8,128)S(1)}, f32[2,256,128]{2,1,0:T(8,128)S(1)}, u32[]{:S(2)}, u32[]{:S(2)}) collective-permute-start(f32[2,256,128]{2,1,0:T(8,128)S(1)} %get-tuple-element.60), channel_id=1, source_target_pairs={{4,0},{8,4},{12,8},{16,12},{20,16},{24,20},{28,24},{5,1},{9,5},{13... | collective-permute-start | bytes 786440 | tf_op jit(solution)/shard_map/ppermute | solution.py:234
  197.2 7.0 %collective-permute-done.13 = f32[2,256,128]{2,1,0:T(8,128)S(1)} collective-permute-done((f32[2,256,128]{2,1,0:T(8,128)S(1)}, f32[2,256,128]{2,1,0:T(8,128)S(1)}, u32[]{:S(2)}, u32[]{:S(2)}) %collective-permute-start.13) | collective-permute-done | bytes 262176 | tf_op jit(solution)/shard_map/ppermute | solution.py:234
  204.2 3.4 %collective-permute-done.14 = f32[2,256,128]{2,1,0:T(8,128)S(1)} collective-permute-done((f32[2,256,128]{2,1,0:T(8,128)S(1)}, f32[2,256,128]{2,1,0:T(8,128)S(1)}, u32[]{:S(2)}, u32[]{:S(2)}) %collective-permute-start.14) | collective-permute-done | bytes 262176 | tf_op jit(solution)/shard_map/ppermute | solution.py:234
  207.5 0.0 collective-permute-done.11
  207.5 0.0 collective-permute-done.12
  207.5 0.2 slice_add_fusion.1
  207.8 1.9 collective-permute-start.15
  209.7 0.1 slice.164
  209.8 0.1 slice.163
  209.9 0.1 slice.166
  210.0 4.3 %collective-permute-start.16 = (f32[2,256,128]{2,1,0:T(8,128)S(1)}, f32[2,256,128]{2,1,0:T(8,128)S(1)}, u32[]{:S(2)}, u32[]{:S(2)}) collective-permute-start(f32[2,256,128]{2,1,0:T(8,128)S(1)} %get-tuple-element.86), channel_id=1, source_target_pairs={{4,0},{8,4},{12,8},{16,12},{20,16},{24,20},{28,24},{5,1},{9,5},{13... | collective-permute-start | bytes 786440 | tf_op jit(solution)/shard_map/ppermute | solution.py:234
  214.3 0.2 pad_maximum_fusion.1
  214.4 0.0 copy-start.13
  214.4 6.5 %collective-permute-done.15 = f32[2,256,128]{2,1,0:T(8,128)S(1)} collective-permute-done((f32[2,256,128]{2,1,0:T(8,128)S(1)}, f32[2,256,128]{2,1,0:T(8,128)S(1)}, u32[]{:S(2)}, u32[]{:S(2)}) %collective-permute-start.15) | collective-permute-done | bytes 262176 | tf_op jit(solution)/shard_map/ppermute | solution.py:234
  220.9 0.1 fusion.1
  221.1 3.4 %collective-permute-done.16 = f32[2,256,128]{2,1,0:T(8,128)S(1)} collective-permute-done((f32[2,256,128]{2,1,0:T(8,128)S(1)}, f32[2,256,128]{2,1,0:T(8,128)S(1)}, u32[]{:S(2)}, u32[]{:S(2)}) %collective-permute-start.16) | collective-permute-done | bytes 262176 | tf_op jit(solution)/shard_map/ppermute | solution.py:234
  224.5 0.1 fusion
  224.6 1.8 multiply_subtract_fusion
  (46 shorter events, 0.3 us)
Async XLA Ops:
  0.0 2.9 %copy-start.12 = (f32[2,512,512]{2,1,0:T(8,128)S(1)}, f32[2,512,512]{2,1,0:T(8,128)}, u32[]{:S(2)}) copy-start(f32[2,512,512]{2,1,0:T(8,128)} %param.15) | copy-start | bytes 6291460
  0.0 13.2 %copy-start.17 = (s32[1,1,24,1]{2,3,1,0:T(1,128)S(1)}, s32[1,1,24,1]{2,3,1,0:T(1,128)}, u32[]{:S(2)}) copy-start(s32[1,1,24,1]{2,3,1,0:T(1,128)} %param.19) | copy-start | bytes 292
  0.0 13.4 %copy-start.16 = (s32[1,1,24,2]{2,3,1,0:T(2,128)S(1)}, s32[1,1,24,2]{2,3,1,0:T(2,128)}, u32[]{:S(2)}) copy-start(s32[1,1,24,2]{2,3,1,0:T(2,128)} %param.18) | copy-start | bytes 580
  3.8 42.1 %collective-permute-start = (f32[2,512,128]{2,1,0:T(8,128)}, f32[2,512,128]{2,1,0:T(8,128)S(1)}, u32[]{:S(2)}, u32[]{:S(2)}) collective-permute-start(f32[2,512,128]{2,1,0:T(8,128)} %get-tuple-element.85), channel_id=1, source_target_pairs={{0,4},{4,8},{8,12},{12,16},{16,20},{20,24},{24,28},{1,5},{5,9},{9,... | collective-permute-start | bytes 1572872 | tf_op jit(solution)/shard_map/ppermute | solution.py:234
  6.9 41.8 %collective-permute-start.1 = (f32[2,512,128]{2,1,0:T(8,128)S(1)}, f32[2,512,128]{2,1,0:T(8,128)S(1)}, u32[]{:S(2)}, u32[]{:S(2)}) collective-permute-start(f32[2,512,128]{2,1,0:T(8,128)S(1)} %get-tuple-element.84), channel_id=1, source_target_pairs={{4,0},{8,4},{12,8},{16,12},{20,16},{24,20},{28,24},{5,1},{9,5},{13... | collective-permute-start | bytes 1572872 | tf_op jit(solution)/shard_map/ppermute | solution.py:234
  9.9 61.0 %collective-permute-start.4 = (f32[3,256,256]{2,1,0:T(8,128)}, f32[3,256,256]{2,1,0:T(8,128)S(1)}, u32[]{:S(2)}, u32[]{:S(2)}) collective-permute-start(f32[3,256,256]{2,1,0:T(8,128)} %get-tuple-element.51), channel_id=1, source_target_pairs={{0,20},{4,16},{8,28},{12,24},{16,4},{20,0},{24,12},{28,8},{1,21},{... | collective-permute-start | bytes 2359304 | tf_op jit(solution)/shard_map/ppermute | solution.py:300
  10.1 77.7 %collective-permute-start.6 = (f32[3,256,256]{2,1,0:T(8,128)}, f32[3,256,256]{2,1,0:T(8,128)S(1)}, u32[]{:S(2)}, u32[]{:S(2)}) collective-permute-start(f32[3,256,256]{2,1,0:T(8,128)} %get-tuple-element.53), channel_id=1, source_target_pairs={{0,16},{4,20},{8,24},{12,28},{16,0},{20,4},{24,8},{28,12},{1,17},{... | collective-permute-start | bytes 2359304 | tf_op jit(solution)/shard_map/ppermute | solution.py:300
  50.5 7.1 %copy-start.14 = (f32[2,512,768]{2,1,0:T(8,128)}, f32[2,512,768]{2,1,0:T(8,128)S(1)}, u32[]{:S(2)}) copy-start(f32[2,512,768]{2,1,0:T(8,128)S(1)} %constant_dynamic-update-slice_fusion) | copy-start | bytes 9437188
  51.9 42.8 %collective-permute-start.2 = (f32[2,128,768]{2,1,0:T(8,128)}, f32[2,128,768]{2,1,0:T(8,128)S(1)}, u32[]{:S(2)}, u32[]{:S(2)}) collective-permute-start(f32[2,128,768]{2,1,0:T(8,128)} %get-tuple-element.82), channel_id=1, source_target_pairs={{0,1},{1,2},{2,3},{4,5},{5,6},{6,7},{8,9},{9,10},{10,11},{12,13},{... | collective-permute-start | bytes 2359304 | tf_op jit(solution)/shard_map/ppermute | solution.py:234
  55.4 41.1 %collective-permute-start.3 = (f32[2,128,768]{2,1,0:T(8,128)}, f32[2,128,768]{2,1,0:T(8,128)S(1)}, u32[]{:S(2)}, u32[]{:S(2)}) collective-permute-start(f32[2,128,768]{2,1,0:T(8,128)} %get-tuple-element.83), channel_id=1, source_target_pairs={{1,0},{2,1},{3,2},{5,4},{6,5},{7,6},{9,8},{10,9},{11,10},{13,12},{... | collective-permute-start | bytes 2359304 | tf_op jit(solution)/shard_map/ppermute | solution.py:234
  70.9 21.1 %copy-start.4 = (f32[3,256,256]{2,1,0:T(8,128)}, f32[3,256,256]{2,1,0:T(8,128)S(1)}, u32[]{:S(2)}) copy-start(f32[3,256,256]{2,1,0:T(8,128)S(1)} %collective-permute-done.4.refs_2_) | copy-start | bytes 2359300
  87.8 4.2 %copy-start.6 = (f32[3,256,256]{2,1,0:T(8,128)}, f32[3,256,256]{2,1,0:T(8,128)S(1)}, u32[]{:S(2)}) copy-start(f32[3,256,256]{2,1,0:T(8,128)S(1)} %collective-permute-done.6.refs_1_) | copy-start | bytes 2359300
  87.8 8.9 %copy-start.15 = (f32[2,512,768]{2,1,0:T(8,128)S(1)}, f32[2,512,768]{2,1,0:T(8,128)}, u32[]{:S(2)}) copy-start(f32[2,512,768]{2,1,0:T(8,128)} %copy-done.14) | copy-start | bytes 9437188
  92.0 27.9 %collective-permute-start.10 = (f32[3,256,256]{2,1,0:T(8,128)S(1)}, f32[3,256,256]{2,1,0:T(8,128)S(1)}, u32[]{:S(2)}, u32[]{:S(2)}) collective-permute-start(f32[3,256,256]{2,1,0:T(8,128)S(1)} %get-tuple-element.68), channel_id=1, source_target_pairs={{0,4},{4,0},{8,12},{12,8},{16,20},{20,16},{24,28},{28,24},{1,5},{5... | collective-permute-start | bytes 2359304 | tf_op jit(solution)/shard_map/ppermute | solution.py:300
  92.1 44.5 %collective-permute-start.8 = (f32[3,256,256]{2,1,0:T(8,128)S(1)}, f32[3,256,256]{2,1,0:T(8,128)S(1)}, u32[]{:S(2)}, u32[]{:S(2)}) collective-permute-start(f32[3,256,256]{2,1,0:T(8,128)S(1)} %get-tuple-element.70), channel_id=1, source_target_pairs={{0,8},{4,12},{8,0},{12,4},{16,24},{20,28},{24,16},{28,20},{1,9},{5... | collective-permute-start | bytes 2359304 | tf_op jit(solution)/shard_map/ppermute | solution.py:300
  92.8 45.2 %collective-permute-start.9 = (f32[3,256,256]{2,1,0:T(8,128)S(1)}, f32[3,256,256]{2,1,0:T(8,128)S(1)}, u32[]{:S(2)}, u32[]{:S(2)}) collective-permute-start(f32[3,256,256]{2,1,0:T(8,128)S(1)} %get-tuple-element.69), channel_id=1, source_target_pairs={{0,12},{4,8},{8,4},{12,0},{16,28},{20,24},{24,20},{28,16},{1,13},{... | collective-permute-start | bytes 2359304 | tf_op jit(solution)/shard_map/ppermute | solution.py:300
  94.7 51.7 %collective-permute-start.7 = (f32[3,256,256]{2,1,0:T(8,128)}, f32[3,256,256]{2,1,0:T(8,128)S(1)}, u32[]{:S(2)}, u32[]{:S(2)}) collective-permute-start(f32[3,256,256]{2,1,0:T(8,128)} %get-tuple-element.71), channel_id=1, source_target_pairs={{0,24},{4,28},{8,16},{12,20},{16,8},{20,12},{24,0},{28,4},{1,25},{... | collective-permute-start | bytes 2359304 | tf_op jit(solution)/shard_map/ppermute | solution.py:300
  96.5 1.0 copy-start.2
  96.5 1.3 copy-start.10
  96.5 1.5 copy-start.11
  96.6 56.9 %collective-permute-start.5 = (f32[3,256,256]{2,1,0:T(8,128)}, f32[3,256,256]{2,1,0:T(8,128)}, u32[]{:S(2)}, u32[]{:S(2)}) collective-permute-start(f32[3,256,256]{2,1,0:T(8,128)} %get-tuple-element.72), channel_id=1, source_target_pairs={{0,28},{4,24},{8,20},{12,16},{16,12},{20,8},{24,4},{28,0},{1,29},{... | collective-permute-start | bytes 2359304 | tf_op jit(solution)/shard_map/ppermute | solution.py:300
  98.1 21.9 %copy-start = (bf16[2,768,256]{2,1,0:T(8,128)(2,1)S(1)}, bf16[2,768,256]{2,1,0:T(8,128)(2,1)}, u32[]{:S(2)}) copy-start(bf16[2,768,256]{2,1,0:T(8,128)(2,1)} %constant.123.clone.refs_5_.refs_3_.refs_2_) | copy-start | bytes 2359300
  98.1 21.9 %copy-start.1 = (bf16[2,256,768]{2,1,0:T(8,128)(2,1)S(1)}, bf16[2,256,768]{2,1,0:T(8,128)(2,1)}, u32[]{:S(2)}) copy-start(bf16[2,256,768]{2,1,0:T(8,128)(2,1)} %constant.125.clone.refs_6_.refs_4_.refs_3_) | copy-start | bytes 2359300
  98.1 21.9 %copy-start.3 = (bf16[512,256]{1,0:T(8,128)(2,1)S(1)}, bf16[512,256]{1,0:T(8,128)(2,1)}, u32[]{:S(2)}) copy-start(bf16[512,256]{1,0:T(8,128)(2,1)} %constant.126.clone.refs_7_.refs_5_.refs_4_) | copy-start | bytes 786436
  98.1 21.9 %copy-start.5 = (f32[3,256,256]{2,1,0:T(8,128)S(1)}, f32[3,256,256]{2,1,0:T(8,128)}, u32[]{:S(2)}) copy-start(f32[3,256,256]{2,1,0:T(8,128)} %copy-done.4) | copy-start | bytes 2359300
  98.1 21.9 %copy-start.7 = (f32[3,256,256]{2,1,0:T(8,128)S(1)}, f32[3,256,256]{2,1,0:T(8,128)}, u32[]{:S(2)}) copy-start(f32[3,256,256]{2,1,0:T(8,128)} %copy-done.6) | copy-start | bytes 2359300
  146.4 0.9 copy-start.8
  147.3 1.1 copy-start.9
  156.8 50.7 %collective-permute-start.11 = (f32[2,128,768]{2,1,0:T(8,128)S(1)}, f32[2,128,768]{2,1,0:T(8,128)S(1)}, u32[]{:S(2)}, u32[]{:S(2)}) collective-permute-start(f32[2,128,768]{2,1,0:T(8,128)S(1)} %get-tuple-element.57), channel_id=1, source_target_pairs={{0,1},{1,2},{2,3},{4,5},{5,6},{6,7},{8,9},{9,10},{10,11},{12,13},{... | collective-permute-start | bytes 2359304 | tf_op jit(solution)/shard_map/ppermute | solution.py:234
  184.5 23.0 %collective-permute-start.12 = (f32[2,128,768]{2,1,0:T(8,128)S(1)}, f32[2,128,768]{2,1,0:T(8,128)S(1)}, u32[]{:S(2)}, u32[]{:S(2)}) collective-permute-start(f32[2,128,768]{2,1,0:T(8,128)S(1)} %get-tuple-element.58), channel_id=1, source_target_pairs={{1,0},{2,1},{3,2},{5,4},{6,5},{7,6},{9,8},{10,9},{11,10},{13,12},{... | collective-permute-start | bytes 2359304 | tf_op jit(solution)/shard_map/ppermute | solution.py:234
  191.0 13.2 %collective-permute-start.13 = (f32[2,256,128]{2,1,0:T(8,128)S(1)}, f32[2,256,128]{2,1,0:T(8,128)S(1)}, u32[]{:S(2)}, u32[]{:S(2)}) collective-permute-start(f32[2,256,128]{2,1,0:T(8,128)S(1)} %get-tuple-element.59), channel_id=1, source_target_pairs={{0,4},{4,8},{8,12},{12,16},{16,20},{20,24},{24,28},{1,5},{5,9},{9,... | collective-permute-start | bytes 786440 | tf_op jit(solution)/shard_map/ppermute | solution.py:234
  192.9 14.6 %collective-permute-start.14 = (f32[2,256,128]{2,1,0:T(8,128)S(1)}, f32[2,256,128]{2,1,0:T(8,128)S(1)}, u32[]{:S(2)}, u32[]{:S(2)}) collective-permute-start(f32[2,256,128]{2,1,0:T(8,128)S(1)} %get-tuple-element.60), channel_id=1, source_target_pairs={{4,0},{8,4},{12,8},{16,12},{20,16},{24,20},{28,24},{5,1},{9,5},{13... | collective-permute-start | bytes 786440 | tf_op jit(solution)/shard_map/ppermute | solution.py:234
  207.8 13.1 %collective-permute-start.15 = (f32[2,256,128]{2,1,0:T(8,128)S(1)}, f32[2,256,128]{2,1,0:T(8,128)S(1)}, u32[]{:S(2)}, u32[]{:S(2)}) collective-permute-start(f32[2,256,128]{2,1,0:T(8,128)S(1)} %get-tuple-element.87), channel_id=1, source_target_pairs={{0,4},{4,8},{8,12},{12,16},{16,20},{20,24},{24,28},{1,5},{5,9},{9,... | collective-permute-start | bytes 786440 | tf_op jit(solution)/shard_map/ppermute | solution.py:234
  210.0 14.5 %collective-permute-start.16 = (f32[2,256,128]{2,1,0:T(8,128)S(1)}, f32[2,256,128]{2,1,0:T(8,128)S(1)}, u32[]{:S(2)}, u32[]{:S(2)}) collective-permute-start(f32[2,256,128]{2,1,0:T(8,128)S(1)} %get-tuple-element.86), channel_id=1, source_target_pairs={{4,0},{8,4},{12,8},{16,12},{20,16},{24,20},{28,24},{5,1},{9,5},{13... | collective-permute-start | bytes 786440 | tf_op jit(solution)/shard_map/ppermute | solution.py:234
  214.4 10.2 %copy-start.13 = (f32[2,512,512]{2,1,0:T(8,128)S(1)}, f32[2,512,512]{2,1,0:T(8,128)}, u32[]{:S(2)}) copy-start(f32[2,512,512]{2,1,0:T(8,128)} %param.15) | copy-start | bytes 6291460
